TPU v7x, 512 devices: a whole 4x8x8 slice. The times are simulated.
512 devices in a mesh: gx: 8 (over z), gy: 4 (over x), gz: 16 (over y, core).
Axes of the slice: x: 4, y: 8, z: 8, core: 2. Of those that a mesh axis runs over, the one named last changes fastest.
Arguments:
- log_perm: float32 [32, 64, 2048], P('gx', 'gy', 'gz'), may hold values from -1 to 1
- pressure: float32 [32, 64, 2048], P('gx', 'gy', 'gz'), may hold values from -4 to 4
- data_weight: float32 [32, 64, 2048], P('gx', 'gy', 'gz'), may hold values from 1 to 30
- probes: float32 [16, 32, 64, 2048], P(None, 'gx', 'gy', 'gz'), may hold values from -3 to 3
Outputs:
- basis: float32 [16, 32, 64, 2048], P(None, 'gx', 'gy', 'gz')
- factor: float32 [16, 16], replicated
All inputs are finite; a program needn't handle non-finite values.
Results may differ from a plain program's by a relative error of at most 0.00029.
Values sent between devices are 32-bit elements; how exact they have to be, the bound alone decides.
No kernel may reach another device: no remote copies, remote signals or barrier semaphores. Data moves between devices by JAX's collectives and lax.ppermute only.
A program may use at most 64 MiB of HBM per device.

v0:
```python
import jax
import jax.numpy as jnp
from jax import lax
from jax.sharding import PartitionSpec as P

DEG = 4


reaction_shift = 0.5
lower_bound = 0.5
upper_bound = 33.5


def padded_2(array, sides, width):
    for axis, dim in sides:
        size, length = (lax.axis_size(axis), array.shape[dim])
        up = [(i, (i + 1) % size) for i in range(size - 1)]
        down = [(j, i) for i, j in up]
        last = lax.slice_in_dim(array, length - width, length, axis=dim)
        first = lax.slice_in_dim(array, 0, width, axis=dim)
        before = lax.ppermute(last, axis, up)
        after = lax.ppermute(first, axis, down)
        array = jnp.concatenate([before, array, after], axis=dim)
    return array


def neighbours(padded):
    return [
        padded[..., 2:, 1:-1, 1:-1],
        padded[..., :-2, 1:-1, 1:-1],
        padded[..., 1:-1, 2:, 1:-1],
        padded[..., 1:-1, :-2, 1:-1],
        padded[..., 1:-1, 1:-1, 2:],
        padded[..., 1:-1, 1:-1, :-2],
    ]


def middle(padded):
    return padded[..., 1:-1, 1:-1, 1:-1]


def operate_padded(field_pad, perm_pad):
    centre = middle(field_pad)
    perm_mid = middle(perm_pad)
    summed = reaction_shift * centre
    for field_nb, perm_nb in zip(neighbours(field_pad), neighbours(perm_pad)):
        summed = summed + 0.5 * (perm_mid + perm_nb) * (centre - field_nb)
    return summed


def forward_term(scaled_pad, press_pad):
    centre = middle(scaled_pad)
    press_mid = middle(press_pad)
    summed = jnp.zeros_like(centre)
    for scaled_nb, press_nb in zip(neighbours(scaled_pad), neighbours(press_pad)):
        summed = summed + 0.5 * (centre + scaled_nb) * (press_mid - press_nb)
    return summed


def adjoint_term(dual_pad, press_pad, permeability):
    centre = middle(dual_pad)
    press_mid = middle(press_pad)
    summed = jnp.zeros_like(centre)
    for dual_nb, press_nb in zip(neighbours(dual_pad), neighbours(press_pad)):
        summed = summed + (centre - dual_nb) * (press_mid - press_nb)
    return 0.5 * permeability * summed


def on_device(log_perm, pressure, data_weight, probes):
    probe_count = probes.shape[0]
    size_x, size_y, size_z = log_perm.shape
    rim_depth = 1
    permeability = jnp.exp(log_perm)
    widened = padded_2(
        jnp.stack([permeability, pressure]), (("gx", 1), ("gy", 2), ("gz", 3)), rim_depth
    )
    perm_pad = widened[0]
    press_pad = widened[1]
    mid_eig = (upper_bound + lower_bound) / 2.0
    half_width = (upper_bound - lower_bound) / 2.0
    ratio_sig = mid_eig / half_width

    def chebyshev(source):
        weight_now = 1.0 / ratio_sig
        residual = source
        direction = source / mid_eig
        iterate = direction
        for repeat in range(DEG):
            direct_pad = padded_2(direction, (("gx", 1), ("gy", 2), ("gz", 3)), 1)
            residual = residual - operate_padded(direct_pad, perm_pad)
            weight_next = 1.0 / (2.0 * ratio_sig - weight_now)
            direction = (
                weight_next * weight_now * direction + 2.0 * weight_next / half_width * residual
            )
            iterate = iterate + direction
            weight_now = weight_next
        return iterate

    scaled_pad = padded_2(permeability[None] * probes, (("gx", 1), ("gy", 2), ("gz", 3)), 1)
    source = forward_term(scaled_pad, press_pad)
    state_field = chebyshev(source)
    dual_field = chebyshev(data_weight[None] * state_field)
    dual_pad = padded_2(dual_field, (("gx", 1), ("gy", 2), ("gz", 3)), 1)
    images = adjoint_term(dual_pad, press_pad, permeability)
    flat_images = images.reshape(probe_count, -1)
    cell_count = (
        size_x * size_y * size_z * lax.axis_size("gx") * lax.axis_size("gy") * lax.axis_size("gz")
    )
    basis_rows = jnp.zeros_like(flat_images)
    factor = jnp.zeros((probe_count, probe_count), jnp.float32)
    for column in range(probe_count):
        column_vec = flat_images[column]
        partial_dots = jnp.dot(
            basis_rows,
            column_vec,
            precision=lax.Precision.HIGHEST,
            preferred_element_type=jnp.float32,
        )
        sums_pair = lax.psum((partial_dots, jnp.sum(column_vec * column_vec)), ("gx", "gy", "gz"))
        coefficients = sums_pair[0] / cell_count
        diagonal_entry = jnp.sqrt(sums_pair[1] / cell_count - jnp.sum(coefficients * coefficients))
        projected = jnp.dot(
            coefficients,
            basis_rows,
            precision=lax.Precision.HIGHEST,
            preferred_element_type=jnp.float32,
        )
        basis_rows = basis_rows.at[column].set((column_vec - projected) / diagonal_entry)
        factor = factor.at[:, column].set(coefficients.at[column].set(diagonal_entry))
    return (basis_rows.reshape(images.shape), factor)


def solution(mesh):
    in_specs = (
        P("gx", "gy", "gz"),
        P("gx", "gy", "gz"),
        P("gx", "gy", "gz"),
        P(None, "gx", "gy", "gz"),
    )
    out_specs = (P(None, "gx", "gy", "gz"), P())
    return jax.shard_map(
        on_device, mesh=mesh, in_specs=in_specs, out_specs=out_specs, check_vma=False
    )
```

profile of v0, /device:TPU:1, one launch (start us, length us, event | category | flops | bytes accessed | tf_op | source)
XLA Modules:
  0.0 1992.0 jit_solution(130361254733294637)
XLA Ops:
  4.0 5.5 collective-permute-start.1
  11.9 4.0 collective-permute-start.3
  17.3 4.6 collective-permute-start.7
  22.1 8.9 collective-permute-start.6
  36.7 4.0 collective-permute-start.9
  43.3 5.3 collective-permute-start.11
  59.6 4.3 collective-permute-start.13
  67.2 4.6 collective-permute-start.15
  91.4 4.7 collective-permute-start.19
  99.4 4.6 collective-permute-start.21
  109.3 4.5 collective-permute-start.23
  126.6 4.7 collective-permute-start.25
  134.7 4.8 collective-permute-start.27
  144.6 4.7 collective-permute-start.29
  162.4 5.6 collective-permute-start.31
  171.3 4.6 collective-permute-start.33
  180.9 4.2 collective-permute-start.35
  198.1 5.9 collective-permute-start.37
  207.3 4.6 collective-permute-start.39
  217.0 4.5 collective-permute-start.41
  234.8 5.9 collective-permute-start.43
  244.0 4.6 collective-permute-start.45
  252.3 4.9 collective-permute-start.47
  270.3 5.9 collective-permute-start.49
  279.4 4.6 collective-permute-start.51
  288.7 4.8 collective-permute-start.53
  305.1 5.9 collective-permute-start.55
  314.3 4.6 collective-permute-start.57
  324.0 4.6 collective-permute-start.59
  341.4 5.9 collective-permute-start.61
  350.6 4.6 collective-permute-start.63
  357.6 4.5 collective-permute-start.65
  379.5 113.1 %all-reduce.17 = (f32[16]{0:T(128)S(1)}, f32[]{:T(128)}) all-reduce(f32[16]{0:T(128)S(1)} %convolution_bitcast_fusion.15, f32[]{:T(128)} %get-tuple-element.585), channel_id=1, replica_groups=mesh['gx'=8,'gy'=4,'gz'=16] {'gx','gy','gz'}, use_global_device_ids=true, to_apply=%region_0.0 | all-reduce | flops 17 | bytes 136 | tf_op jit(solution)/shard_map/psum | solution.py:119
  495.6 94.9 %all-reduce.16 = (f32[16]{0:T(128)S(1)}, f32[]{:T(128)}) all-reduce(f32[16]{0:T(128)S(1)} %convolution_bitcast_fusion.14, f32[]{:T(128)} %get-tuple-element.586), channel_id=1, replica_groups=mesh['gx'=8,'gy'=4,'gz'=16] {'gx','gy','gz'}, use_global_device_ids=true, to_apply=%region_4.0 | all-reduce | flops 17 | bytes 136 | tf_op jit(solution)/shard_map/psum | solution.py:119
  593.6 95.2 %all-reduce.15 = (f32[16]{0:T(128)S(1)}, f32[]{:T(128)}) all-reduce(f32[16]{0:T(128)S(1)} %convolution_bitcast_fusion.13, f32[]{:T(128)} %get-tuple-element.587), channel_id=1, replica_groups=mesh['gx'=8,'gy'=4,'gz'=16] {'gx','gy','gz'}, use_global_device_ids=true, to_apply=%region_8.0 | all-reduce | flops 17 | bytes 136 | tf_op jit(solution)/shard_map/psum | solution.py:119
  692.0 95.2 %all-reduce.14 = (f32[16]{0:T(128)S(1)}, f32[]{:T(128)}) all-reduce(f32[16]{0:T(128)S(1)} %convolution_bitcast_fusion.12, f32[]{:T(128)} %get-tuple-element.588), channel_id=1, replica_groups=mesh['gx'=8,'gy'=4,'gz'=16] {'gx','gy','gz'}, use_global_device_ids=true, to_apply=%region_12.0 | all-reduce | flops 17 | bytes 136 | tf_op jit(solution)/shard_map/psum | solution.py:119
  790.5 96.1 %all-reduce.13 = (f32[16]{0:T(128)S(1)}, f32[]{:T(128)}) all-reduce(f32[16]{0:T(128)S(1)} %convolution_bitcast_fusion.11, f32[]{:T(128)} %get-tuple-element.589), channel_id=1, replica_groups=mesh['gx'=8,'gy'=4,'gz'=16] {'gx','gy','gz'}, use_global_device_ids=true, to_apply=%region_16.0 | all-reduce | flops 17 | bytes 136 | tf_op jit(solution)/shard_map/psum | solution.py:119
  889.9 95.5 %all-reduce.12 = (f32[16]{0:T(128)S(1)}, f32[]{:T(128)}) all-reduce(f32[16]{0:T(128)S(1)} %convolution_bitcast_fusion.10, f32[]{:T(128)} %get-tuple-element.590), channel_id=1, replica_groups=mesh['gx'=8,'gy'=4,'gz'=16] {'gx','gy','gz'}, use_global_device_ids=true, to_apply=%region_20.0 | all-reduce | flops 17 | bytes 136 | tf_op jit(solution)/shard_map/psum | solution.py:119
  988.7 96.0 %all-reduce.11 = (f32[16]{0:T(128)S(1)}, f32[]{:T(128)}) all-reduce(f32[16]{0:T(128)S(1)} %convolution_bitcast_fusion.9, f32[]{:T(128)} %get-tuple-element.591), channel_id=1, replica_groups=mesh['gx'=8,'gy'=4,'gz'=16] {'gx','gy','gz'}, use_global_device_ids=true, to_apply=%region_24.0 | all-reduce | flops 17 | bytes 136 | tf_op jit(solution)/shard_map/psum | solution.py:119
  1088.1 95.3 %all-reduce.10 = (f32[16]{0:T(128)S(1)}, f32[]{:T(128)}) all-reduce(f32[16]{0:T(128)S(1)} %convolution_bitcast_fusion.8, f32[]{:T(128)} %get-tuple-element.592), channel_id=1, replica_groups=mesh['gx'=8,'gy'=4,'gz'=16] {'gx','gy','gz'}, use_global_device_ids=true, to_apply=%region_28.0 | all-reduce | flops 17 | bytes 136 | tf_op jit(solution)/shard_map/psum | solution.py:119
  1186.6 96.2 %all-reduce.9 = (f32[16]{0:T(128)S(1)}, f32[]{:T(128)}) all-reduce(f32[16]{0:T(128)S(1)} %convolution_bitcast_fusion.7, f32[]{:T(128)} %get-tuple-element.593), channel_id=1, replica_groups=mesh['gx'=8,'gy'=4,'gz'=16] {'gx','gy','gz'}, use_global_device_ids=true, to_apply=%region_32.0 | all-reduce | flops 17 | bytes 136 | tf_op jit(solution)/shard_map/psum | solution.py:119
  1286.0 95.4 %all-reduce.8 = (f32[16]{0:T(128)S(1)}, f32[]{:T(128)}) all-reduce(f32[16]{0:T(128)S(1)} %convolution_bitcast_fusion.6, f32[]{:T(128)} %get-tuple-element.594), channel_id=1, replica_groups=mesh['gx'=8,'gy'=4,'gz'=16] {'gx','gy','gz'}, use_global_device_ids=true, to_apply=%region_36.0 | all-reduce | flops 17 | bytes 136 | tf_op jit(solution)/shard_map/psum | solution.py:119
  1384.7 96.2 %all-reduce.7 = (f32[16]{0:T(128)S(1)}, f32[]{:T(128)}) all-reduce(f32[16]{0:T(128)S(1)} %convolution_bitcast_fusion.5, f32[]{:T(128)} %get-tuple-element.595), channel_id=1, replica_groups=mesh['gx'=8,'gy'=4,'gz'=16] {'gx','gy','gz'}, use_global_device_ids=true, to_apply=%region_40.0 | all-reduce | flops 17 | bytes 136 | tf_op jit(solution)/shard_map/psum | solution.py:119
  1484.2 95.3 %all-reduce.6 = (f32[16]{0:T(128)S(1)}, f32[]{:T(128)}) all-reduce(f32[16]{0:T(128)S(1)} %convolution_bitcast_fusion.4, f32[]{:T(128)} %get-tuple-element.596), channel_id=1, replica_groups=mesh['gx'=8,'gy'=4,'gz'=16] {'gx','gy','gz'}, use_global_device_ids=true, to_apply=%region_44.0 | all-reduce | flops 17 | bytes 136 | tf_op jit(solution)/shard_map/psum | solution.py:119
  1582.9 96.2 %all-reduce.5 = (f32[16]{0:T(128)S(1)}, f32[]{:T(128)}) all-reduce(f32[16]{0:T(128)S(1)} %convolution_bitcast_fusion.3, f32[]{:T(128)} %get-tuple-element.597), channel_id=1, replica_groups=mesh['gx'=8,'gy'=4,'gz'=16] {'gx','gy','gz'}, use_global_device_ids=true, to_apply=%region_48.0 | all-reduce | flops 17 | bytes 136 | tf_op jit(solution)/shard_map/psum | solution.py:119
  1682.3 95.3 %all-reduce.4 = (f32[16]{0:T(128)S(1)}, f32[]{:T(128)}) all-reduce(f32[16]{0:T(128)S(1)} %convolution_bitcast_fusion.2, f32[]{:T(128)} %get-tuple-element.598), channel_id=1, replica_groups=mesh['gx'=8,'gy'=4,'gz'=16] {'gx','gy','gz'}, use_global_device_ids=true, to_apply=%region_52.0 | all-reduce | flops 17 | bytes 136 | tf_op jit(solution)/shard_map/psum | solution.py:119
  1780.8 96.2 %all-reduce.3 = (f32[16]{0:T(128)S(1)}, f32[]{:T(128)}) all-reduce(f32[16]{0:T(128)S(1)} %convolution_bitcast_fusion.1, f32[]{:T(128)} %get-tuple-element.599), channel_id=1, replica_groups=mesh['gx'=8,'gy'=4,'gz'=16] {'gx','gy','gz'}, use_global_device_ids=true, to_apply=%region_56.0 | all-reduce | flops 17 | bytes 136 | tf_op jit(solution)/shard_map/psum | solution.py:119
  1880.2 95.4 %all-reduce.2 = (f32[16]{0:T(128)S(1)}, f32[]{:T(128)}) all-reduce(f32[16]{0:T(128)S(1)} %convolution_bitcast_fusion, f32[]{:T(128)} %get-tuple-element.584), channel_id=1, replica_groups=mesh['gx'=8,'gy'=4,'gz'=16] {'gx','gy','gz'}, use_global_device_ids=true, to_apply=%region_60.0 | all-reduce | flops 17 | bytes 136 | tf_op jit(solution)/shard_map/psum | solution.py:119
  (440 shorter events, 261.2 us)
Async XLA Ops:
  2.8 7.8 collective-permute-start.2
  4.0 6.6 collective-permute-start.1
  10.6 11.3 collective-permute-start.4
  11.9 10.0 collective-permute-start.3
  16.0 19.3 collective-permute-start
  17.3 18.0 collective-permute-start.7
  22.1 10.9 collective-permute-start.6
  35.4 6.0 collective-permute-start.8
  43.3 8.7 collective-permute-start.11
  58.3 6.0 collective-permute-start.12
  59.6 6.2 collective-permute-start.13
  65.9 5.9 collective-permute-start.14
  76.5 6.3 collective-permute-start.17
  90.1 6.4 collective-permute-start.18
  91.4 6.6 collective-permute-start.19
  98.1 5.9 collective-permute-start.20
  109.3 7.7 collective-permute-start.23
  125.3 6.5 collective-permute-start.24
  126.6 6.7 collective-permute-start.25
  133.4 6.1 collective-permute-start.26
  144.6 8.0 collective-permute-start.29
  161.1 7.3 collective-permute-start.30
  162.4 7.5 collective-permute-start.31
  170.0 5.9 collective-permute-start.32
  180.9 8.0 collective-permute-start.35
  196.8 7.7 collective-permute-start.36
  198.1 7.9 collective-permute-start.37
  206.0 5.9 collective-permute-start.38
  217.0 8.3 collective-permute-start.41
  233.5 7.6 collective-permute-start.42
  234.8 7.8 collective-permute-start.43
  242.7 5.9 collective-permute-start.44
  252.3 8.7 collective-permute-start.47
  269.0 7.6 collective-permute-start.48
  270.3 7.8 collective-permute-start.49
  278.1 5.9 collective-permute-start.50
  279.4 5.8 collective-permute-start.51
  288.7 7.5 collective-permute-start.53
  303.8 7.6 collective-permute-start.54
  305.1 7.8 collective-permute-start.55
  313.0 5.9 collective-permute-start.56
  324.0 8.4 collective-permute-start.59
  340.1 7.6 collective-permute-start.60
  341.4 7.8 collective-permute-start.61
  349.3 6.0 collective-permute-start.62
  350.6 5.8 collective-permute-start.63
  357.6 17.4 collective-permute-start.65
  362.8 13.0 collective-permute-start.64
  (65 other events, 630.6 us)
where the time goes:
time: 2010 us; the launch traced here: 1990 us
  blocking collectives  1550 us (77%)
  starting transfers between devices  213 us (11%)
  local copies, waits for them, and re-layouts  81.1 us (4%)
  other arithmetic  61.6 us (3%)
  waiting for transfers between devices  47 us (2%)
  between operations  24 us (1%)
    psum x16, blocking collectives, on_device(): lax.psum((partial_dots, jnp.sum(column_vec * column_vec)), ('gx', 'gy', '...  1550 us
    ppermute x33, starting transfers between devices, padded_2(): before = lax.ppermute(last, axis, up)  156 us
    ppermute x33, starting transfers between devices, padded_2(): after = lax.ppermute(first, axis, down)  57.4 us
  transfers between devices with their start and end apart: 66, of which 38 were waited for; matrix products, arithmetic and copies ran while one was open for 2% of the time, Pallas kernels for 0%

commit v1 on v0

v1 whole, which is shorter than its diff:
```python
import jax
import jax.numpy as jnp
from jax import lax
from jax.experimental import pallas as pl
from jax.experimental.pallas import tpu as pltpu
from jax.sharding import PartitionSpec as P

DEG = 4
SHIFT = 0.5
LOWER = 0.5
UPPER = 33.5
MID = (UPPER + LOWER) / 2.0
HALF = (UPPER - LOWER) / 2.0
RATIO = MID / HALF

PROBES = 16
CELLS = 32 * 64 * 2048
WIN = 16
HALO = 2 * DEG + 2
INNER = DEG + 1
ROWS = WIN + 2 * HALO
UNROLL = 4
MSG = 12 * HALO + 4 * INNER
F32 = jnp.float32


def lane_sub():
    lane = lax.broadcasted_iota(jnp.int32, (8, 128), 1)
    return lane, lax.broadcasted_iota(jnp.int32, (8, 128), 0)


def swap_groups(v):
    lane, _ = lane_sub()
    high, low = (lane & 64) == 0, (lane & 32) == 0
    u = [None] * 4
    for a in range(2):
        u[a] = jnp.where(high, v[a], pltpu.roll(v[a + 2], 64, 1))
        u[a + 2] = jnp.where(high, pltpu.roll(v[a], 64, 1), v[a + 2])
    out = [None] * 4
    for a in (0, 2):
        out[a] = jnp.where(low, u[a], pltpu.roll(u[a + 1], 32, 1))
        out[a + 1] = jnp.where(low, pltpu.roll(u[a], 96, 1), u[a + 1])
    return out


def x_up(v):
    return [pltpu.roll(v[n - 3], 7, 0) if n % 4 == 3 else v[n + 1] for n in range(8)]


def y_up(v):
    return [v[n + 4] if n < 4 else pltpu.roll(v[n - 4], 124, 1) for n in range(8)]


def pack_kernel(lp_ref, pr_ref, dw_ref, v_ref, out_ref, perm_ref, mix_ref):
    perm_ref[...] = jnp.exp(lp_ref[...])
    first = (lane_sub()[0] & 2) == 0

    def mixed(parts):
        for slot in range(4):
            mix_ref[pl.ds(slot, 32, stride=4), :] = parts[slot]
        return mix_ref[...].T

    def half(ref, yl):
        return ref[pl.ds(yl, 32, stride=2), :]

    def paired(tile, w):
        return jnp.where(first, tile[16 * w : 16 * w + 8], tile[16 * w + 8 : 16 * w + 16])

    for yl in range(2):
        perm = half(perm_ref, yl)
        for q in range(4):
            tile = mixed([perm * v_ref[4 * q + p, pl.ds(yl, 32, stride=2), :] for p in range(4)])
            for w in range(8):
                out_ref[4 * w + q, 16 * yl : 16 * yl + 16] = tile[16 * w : 16 * w + 16]
        tile = mixed([perm, half(pr_ref, yl)] * 2)
        for w in range(8):
            packed = paired(tile, w)
            for q in range(4):
                out_ref[4 * w + q, 32 + 8 * yl : 40 + 8 * yl] = packed
    tile = mixed([half(dw_ref, 0), half(dw_ref, 1)] * 2)
    for w in range(8):
        packed = paired(tile, w)
        for q in range(4):
            out_ref[4 * w + q, 48:56] = packed


def widen(v, first):
    return jnp.where(first, v, pltpu.roll(v, 2, 1)), jnp.where(first, pltpu.roll(v, 126, 1), v)


def split(v, even):
    return jnp.where(even, v, pltpu.roll(v, 1, 1)), jnp.where(even, pltpu.roll(v, 127, 1), v)


def arrange_kernel(in_ref, s_ref, c_ref, w_ref, low_ref, high_ref):
    lane, _ = lane_sub()
    first = (lane & 2) == 0

    def fetch(rows):
        got = [[in_ref[pl.ds(56 * g + row, 8, stride=224), :] for g in range(4)] for row in rows]
        return [swap_groups(v) for v in got]

    lift, pairs = WIN - HALO, HALO // 2
    for yl in range(2):
        for batch in range(0, WIN, 8):
            got = fetch([16 * yl + batch + k for k in range(8)])
            for k in range(8):
                z = batch + k
                for x, v in enumerate(got[k]):
                    n = 4 * yl + x
                    s_ref[z, n] = v
                    if z < HALO:
                        low_ref[8 * z + n] = v
                    if z >= lift:
                        high_ref[8 * (z - lift) + n] = v
        got = fetch([32 + 8 * yl + z for z in range(8)])
        for x in range(4):
            n = 4 * yl + x
            wide = [widen(got[z][x], first) for z in range(8)]
            c = [v[0] for v in wide] + [v[1] for v in wide]
            for z in range(WIN):
                c_ref[z, n] = c[z]
            for k in range(pairs):
                at = 8 * HALO + 8 * k + n
                low_ref[at] = jnp.where(first, c[k], c[k + pairs])
                high_ref[at] = jnp.where(first, c[lift + k], c[lift + k + pairs])
    got = fetch([48 + z for z in range(8)])
    wide = [[widen(v, first) for v in got[z]] for z in range(8)]
    for z in range(8):
        for x in range(4):
            below, above = wide[z][x]
            w_ref[z, x] = below
            w_ref[z + 8, x] = above
            if z < INNER:
                low_ref[12 * HALO + 4 * z + x] = below
            if z + 8 >= WIN - INNER:
                high_ref[12 * HALO + 4 * (z + 8 - WIN + INNER) + x] = above


def core_kernel(
    edge_ref, lo_ref, s_own_ref, c_own_ref, w_own_ref, hi_ref, out_ref,
    kx_ref, ky_ref, kz_ref, kd_ref, diag_ref, dx_ref, dy_ref, dz_ref, dd_ref, pd_ref,
    perm_ref, press_ref, wt_ref, s_ref, r_ref, e0_ref, e1_ref, z_ref,
):
    lane, sub = lane_sub()
    first, even = (lane & 2) == 0, (lane & 1) == 0
    at_first, at_last = edge_ref[0], edge_ref[1]

    def fill(k, base, inner, s, c, w, count):
        c = [split(v, even) for v in c]
        w = [split(v, even) for v in w]
        for n in range(8 * count):
            if s:
                s_ref[base + n // 8, n % 8] = s[n]
        for n in range(len(c)):
            perm_ref[base + n // 8, n % 8], press_ref[base + n // 8, n % 8] = c[n]
        for n in range(len(w)):
            row, x = inner + n // 4, n % 4
            wt_ref[row, x], wt_ref[row, 4 + x] = w[n]

    def fill_own(i, carry):
        k = 2 * i
        s = [s_own_ref[k + n // 8, n % 8] for n in range(16)]
        c = [c_own_ref[k + n // 8, n % 8] for n in range(16)]
        w = [w_own_ref[k + n // 4, n % 4] for n in range(8)]
        fill(k, HALO + k, INNER + k, s, c, w, 2)
        return carry

    lax.fori_loop(0, WIN // 2, fill_own, 0)
    pairs = HALO // 2
    for src_ref, base, inner in ((lo_ref, 0, 0), (hi_ref, HALO + WIN, INNER + WIN)):
        for k in range(HALO):
            for n in range(8):
                s_ref[base + k, n] = src_ref[8 * k + n]
        wide = [widen(src_ref[8 * HALO + i], first) for i in range(8 * pairs)]
        w = [src_ref[12 * HALO + i] for i in range(4 * INNER)]
        fill(0, base, inner, [], [v[0] for v in wide], w, 0)
        fill(0, base + pairs, inner, [], [v[1] for v in wide], [], 0)

    def mark(n):
        none = jnp.zeros((8, 128), F32)
        return (
            jnp.where(sub == 0, 0.5, 0.0) if n % 4 == 0 else none,
            jnp.where(sub == 7, 0.5, 0.0) if n % 4 == 3 else none,
            jnp.where(lane < 4, 0.5, 0.0) if n < 4 else none,
            jnp.where(lane >= 124, 0.5, 0.0) if n >= 4 else none,
        )

    ends = [mark(n) for n in range(8)]

    def coefficients(row, carry):
        here, above = jnp.int32(row == HALO), jnp.int32(row == HALO + WIN - 1)
        below = jnp.int32(row == HALO - 1)
        out_z = 0.5 * (here * at_first + above * at_last).astype(F32)
        half_z = 0.5 * (1 - below * at_first - above * at_last).astype(F32)
        perm = [perm_ref[row, n] for n in range(8)]
        press = [press_ref[row, n] for n in range(8)]
        perm_z = [perm_ref[row + 1, n] for n in range(8)]
        press_z = [press_ref[row + 1, n] for n in range(8)]
        perm_x, perm_y, press_x, press_y = x_up(perm), y_up(perm), x_up(press), y_up(press)
        outs = []
        for n in range(8):
            x_begin, x_end, y_begin, y_end = ends[n]
            outside = (x_begin + x_end) + (y_begin + y_end) + out_z
            half_x, half_y = 0.5 - x_end, 0.5 - y_end
            outs.append((kx_ref, n, half_x * (perm[n] + perm_x[n])))
            outs.append((ky_ref, n, half_y * (perm[n] + perm_y[n])))
            outs.append((kz_ref, n, half_z * (perm[n] + perm_z[n])))
            outs.append((diag_ref, n, SHIFT + outside * perm[n]))
            outs.append((dx_ref, n, half_x * (press[n] - press_x[n])))
            outs.append((dy_ref, n, half_y * (press[n] - press_y[n])))
            outs.append((dz_ref, n, half_z * (press[n] - press_z[n])))
            outs.append((pd_ref, n, outside * press[n]))
        lower = x_far(perm, press) + y_far(perm, press)
        for i, n in enumerate((0, 4, 0, 1, 2, 3)):
            half = 0.5 - ends[n][0 if i < 2 else 2]
            outs.append((kd_ref, i, half * (perm[n] + lower[i][0])))
            outs.append((dd_ref, i, half * (lower[i][1] - press[n])))
        for ref, n, value in outs:
            ref[row, n] = value
        return carry

    def x_far(a, b):
        return [(pltpu.roll(a[n + 3], 1, 0), pltpu.roll(b[n + 3], 1, 0)) for n in (0, 4)]

    def y_far(a, b):
        return [(pltpu.roll(a[n + 4], 4, 1), pltpu.roll(b[n + 4], 4, 1)) for n in range(4)]

    lax.fori_loop(0, ROWS - 1, coefficients, 0)

    def load(ref, row, count=8):
        return [ref[row, n] for n in range(count)]

    def far(v):
        return (
            [pltpu.roll(v[n], 7, 0) for n in (0, 4)]
            + [pltpu.roll(v[n], 1, 0) for n in (3, 7)]
            + [pltpu.roll(v[n], 124, 1) for n in range(4)]
            + [pltpu.roll(v[n + 4], 4, 1) for n in range(4)]
        )

    def sweep(field_ref, begin, end, face_refs, centre_ref, join, sign, inputs, finish):
        fx_ref, fy_ref, fz_ref, fd_ref = face_refs

        def part(up, down):
            return up - down if sign < 0 else up + down

        def rows(row, count, carry):
            now, around, before = carry
            results = []
            for u in range(count):
                later = load(field_ref, row + u + 1)
                later_around = far(later)
                fx, fy, fz = (load(ref, row + u) for ref in (fx_ref, fy_ref, fz_ref))
                fd, centre = load(fd_ref, row + u, 6), load(centre_ref, row + u)
                flow_x, back_x, flow_y, back_y = ([None] * 8 for _ in range(4))
                for n in range(8):
                    up = now[n + 1] if n % 4 < 3 else around[n // 4]
                    flow_x[n] = join(now[n], up) * fx[n]
                    up = now[n + 4] if n < 4 else around[n]
                    flow_y[n] = join(now[n], up) * fy[n]
                for n in range(8):
                    if n % 4:
                        back_x[n] = flow_x[n - 1]
                    else:
                        back_x[n] = join(around[2 + n // 4], now[n]) * fd[n // 4]
                    if n >= 4:
                        back_y[n] = flow_y[n - 4]
                    else:
                        back_y[n] = join(around[8 + n], now[n]) * fd[2 + n]
                flow_z = [join(now[n], later[n]) * fz[n] for n in range(8)]
                for n in range(8):
                    total = centre[n] * now[n] + part(flow_x[n], back_x[n])
                    total = total + (part(flow_y[n], back_y[n]) + part(flow_z[n], before[n]))
                    extra = [ref[row + u, n] for ref in inputs]
                    results.append((row + u, n, finish(row + u, n, now[n], total, *extra)))
                now, around, before = later, later_around, flow_z
            for at, n, outs in results:
                for put, value in outs:
                    put(at, n, value)
            return now, around, before

        now, later = load(field_ref, begin - 1), load(field_ref, begin)
        fz = load(fz_ref, begin - 1)
        carry = later, far(later), [join(now[n], later[n]) * fz[n] for n in range(8)]
        steps, rest = divmod(end - begin, UNROLL)
        carry = lax.fori_loop(
            0, steps, lambda i, c: rows(begin + UNROLL * i, UNROLL, c), carry
        )
        if rest:
            rows(end - rest, rest, carry)

    def add(a, b):
        return a + b

    def minus(a, b):
        return a - b

    def into(ref):
        def put(row, n, value):
            ref[row, n] = value

        return put

    def start(value):
        direction = value * (1.0 / MID)
        return [(into(r_ref), value), (into(e0_ref), direction), (into(z_ref), direction)]

    def solve(lowest, finish_last):
        weight_now = 1.0 / RATIO
        here, there = e0_ref, e1_ref
        for repeat in range(DEG):
            weight_next = 1.0 / (2.0 * RATIO - weight_now)
            keep, take = weight_next * weight_now, 2.0 * weight_next / HALF
            weight_now = weight_next
            last = repeat == DEG - 1

            def finish(row, n, v, total, residual, iterate, k=keep, m=take, to=there, last=last):
                residual = residual - total
                direction = k * v + m * residual
                iterate = iterate + direction
                if last:
                    return finish_last(row, n, iterate)
                return [(into(r_ref), residual), (into(to), direction), (into(z_ref), iterate)]

            begin = lowest + 1 + repeat
            faces = (kx_ref, ky_ref, kz_ref, kd_ref)
            sweep(here, begin, ROWS - begin, faces, diag_ref, minus, -1, (r_ref, z_ref), finish)
            here, there = there, here

    faces = (dx_ref, dy_ref, dz_ref, dd_ref)
    sweep(
        s_ref, 1, ROWS - 1, faces, pd_ref, add, -1, (), lambda row, n, v, total: start(total)
    )
    skip = HALO - INNER
    solve(1, lambda row, n, value: start(value * wt_ref[row - skip, n]))
    solve(skip, lambda row, n, value: [(into(s_ref), value)])

    def image(row, n, v, total):
        return [(into(z_ref), perm_ref[row, n] * total)]

    sweep(s_ref, HALO, HALO + WIN, faces, pd_ref, minus, 1, (), image)

    def send(i, carry):
        got = [
            (4 * i + k, yl, [z_ref[HALO + 4 * i + k, 4 * yl + x] for x in range(4)])
            for k in range(4)
            for yl in range(2)
        ]
        for k, yl, v in [(k, yl, swap_groups(v)) for k, yl, v in got]:
            for g in range(4):
                out_ref[pl.ds(g * 2 * WIN + yl * WIN + k, 8, stride=8 * WIN), :] = v[g]
        return carry

    lax.fori_loop(0, WIN // 4, send, 0)


def gram_kernel(in_ref, img_ref, gram_ref, acc_ref, mix_ref):
    for q in range(4):
        for yl in range(2):
            rows = [in_ref[4 * w + q, 16 * yl : 16 * yl + 16] for w in range(8)]
            mix_ref[...] = jnp.concatenate(rows, axis=0).T
            for p in range(4):
                img_ref[4 * q + p, pl.ds(yl, 32, stride=2), :] = mix_ref[pl.ds(p, 32, stride=4), :]
    for i in range(PROBES):
        a = [img_ref[i, 8 * k : 8 * k + 8] for k in range(8)]
        for j in range(i + 1):
            parts = [a[k] * img_ref[j, 8 * k : 8 * k + 8] for k in range(8)]
            while len(parts) > 1:
                parts = [parts[k] + parts[k + 1] for k in range(0, len(parts), 2)]
            begin = (16 * i + j) * 8
            acc_ref[begin : begin + 8] = parts[0]
            begin = (16 * j + i) * 8
            acc_ref[begin : begin + 8] = parts[0]
    sums = []
    for c in range(32):
        parts = [acc_ref[pl.ds(64 * c + s, 8, stride=8), :] for s in range(8)]
        while len(parts) > 1:
            parts = [parts[k] + parts[k + 1] for k in range(0, len(parts), 2)]
        sums.append(parts[0])
    total = lax.dot_general(
        jnp.ones((8, 128), F32),
        jnp.concatenate(sums, axis=0),
        (((1,), (1,)), ((), ())),
        precision=lax.Precision.HIGHEST,
        preferred_element_type=F32,
    )
    _, sub = lane_sub()
    tile = jnp.where(sub == 0, total[:, :128], total[:, 128:])
    for d in range(32):
        gram_ref[d] = tile


def spread_kernel(in_ref, out_ref):
    total = jnp.sum(in_ref[...], axis=0)
    for d in range(16):
        out_ref[d] = total


def finish_kernel(gram_ref, img_ref, out_ref, factor_ref, inv_ref):
    total = jnp.sum(gram_ref[...], axis=0) * (1.0 / CELLS)
    lane = lax.broadcasted_iota(jnp.int32, (16, 128), 1)
    row = lax.broadcasted_iota(jnp.int32, (16, 128), 0)
    g = jnp.concatenate(
        [jnp.broadcast_to(total[0:1], (8, 128)), jnp.broadcast_to(total[1:2], (8, 128))], axis=0
    )
    g = jnp.where((lane >> 4) == (row & 7), g, 0.0)
    for step in (16, 32, 64):
        g = g + pltpu.roll(g, step, 1)
    g = jnp.where(lane < 16, g, jnp.where(lane == row + 16, 1.0, 0.0))
    for k in range(PROBES - 1):
        pivot_row = jnp.broadcast_to(g[k : k + 1], (16, 128))
        column = jnp.broadcast_to(g[:, k : k + 1], (16, 128))
        pivot = jnp.broadcast_to(pivot_row[:, k : k + 1], (16, 128))
        g = g - jnp.where(row > k, column / pivot, 0.0) * pivot_row
    diagonal = jnp.sum(jnp.where(lane == row, g, 0.0), axis=1, keepdims=True)
    g = g / jnp.sqrt(diagonal)
    factor_ref[...] = jnp.where(lane >= row, g, 0.0)[:, :16]
    for j in range(PROBES):
        inv_ref[j] = jnp.broadcast_to(g[:, 16 + j : 17 + j], (16, 128))
    for i in range(PROBES):
        scale = [jnp.broadcast_to(inv_ref[j, i : i + 1], (8, 128)) for j in range(i + 1)]
        for k in range(8):
            value = scale[0] * img_ref[0, 8 * k : 8 * k + 8]
            for j in range(1, i + 1):
                value = value + scale[j] * img_ref[j, 8 * k : 8 * k + 8]
            out_ref[i, 8 * k : 8 * k + 8] = value


def call(kernel, out_shapes, scratch=(), smem=0, inputs=1):
    out_shape = [jax.ShapeDtypeStruct(s, F32) for s in out_shapes]
    vmem = pl.BlockSpec(memory_space=pltpu.VMEM)
    specs = [pl.BlockSpec(memory_space=pltpu.SMEM)] * smem + [vmem] * inputs
    return pl.pallas_call(
        kernel,
        out_shape=out_shape,
        in_specs=specs,
        out_specs=[vmem] * len(out_shape),
        scratch_shapes=[pltpu.VMEM(s, F32) for s in scratch],
        compiler_params=pltpu.CompilerParams(vmem_limit_bytes=40 * 1024 * 1024),
    )


def on_device(log_perm, pressure, data_weight, probes):
    planes = [a.reshape(64, 128) for a in (log_perm, pressure, data_weight)]
    (sent,) = call(pack_kernel, [(32, 56, 128)], [(64, 128), (128, 128)], inputs=4)(
        *planes, probes.reshape(16, 64, 128)
    )
    got = lax.all_to_all(sent, ("gx", "gy"), 0, 0)
    plane, msg = (WIN, 8, 8, 128), (MSG, 8, 128)
    own_s, own_c, own_w, low, high = call(
        arrange_kernel, [plane, plane, (WIN, 4, 8, 128), msg, msg]
    )(got.reshape(32 * 56, 128))

    size_x, size_z = lax.axis_size("gx"), lax.axis_size("gz")

    def place(n):
        return (n % size_x) * size_z + n // size_x

    count = size_x * size_z
    up = [(place(n), place(n + 1)) for n in range(count - 1)]
    down = [(j, i) for i, j in up]
    from_below = lax.ppermute(high, ("gx", "gz"), up)
    from_above = lax.ppermute(low, ("gx", "gz"), down)
    number = lax.axis_index("gz") * size_x + lax.axis_index("gx")
    edge = jnp.stack([number == 0, number == count - 1]).astype(jnp.int32)
    field = (ROWS, 8, 8, 128)
    far = (ROWS, 6, 8, 128)
    scratch = ([field] * 3 + [far, field]) * 2
    scratch += [field] * 2 + [(WIN + 2 * INNER, 8, 8, 128)] + [field] * 5
    (images,) = call(core_kernel, [(1024, 128)], scratch, smem=1, inputs=5)(
        edge, from_below, own_s, own_c, own_w, from_above
    )
    back = lax.all_to_all(images.reshape(32, 32, 128), ("gx", "gy"), 0, 0)
    image_rows, gram = call(gram_kernel, [(16, 64, 128), (32, 8, 128)], [(2048, 128), (128, 128)])(back)
    gram = lax.all_to_all(gram, ("gx", "gy"), 0, 0)
    (gram,) = call(spread_kernel, [(16, 8, 128)])(gram)
    gram = lax.all_to_all(gram, "gz", 0, 0)
    basis, factor = call(
        finish_kernel, [(16, 64, 128), (16, 16)], [(16, 16, 128)], inputs=2
    )(gram, image_rows)
    return (basis.reshape(probes.shape), factor)


def solution(mesh):
    in_specs = (
        P("gx", "gy", "gz"),
        P("gx", "gy", "gz"),
        P("gx", "gy", "gz"),
        P(None, "gx", "gy", "gz"),
    )
    out_specs = (P(None, "gx", "gy", "gz"), P())
    return jax.shard_map(
        on_device, mesh=mesh, in_specs=in_specs, out_specs=out_specs, check_vma=False
    )
```

time: 2010 us -> 139 us (0.07)
  blocking collectives: 1550 us -> 91.8 us
  starting transfers between devices: 213 us -> 7.06 us
  local copies, waits for them, and re-layouts: 81.1 us -> 3.31 us
  other arithmetic: 61.6 us -> 0.08 us
  waiting for transfers between devices: 47 us -> 12.7 us
  between operations: 24 us -> 0.69 us
  Pallas kernels: 0 us -> 22.6 us
    psum x16 -> x0, blocking collectives: 1550 us -> none  [on_device(): lax.psum((partial_dots, jnp.sum(column_vec * column_vec)), ('gx', 'gy', '...]
    ppermute x66 -> x2, starting transfers between devices: 213 us -> 7.06 us  [the longest x1 4.52 us: on_device(): from_above = lax.ppermute(low, ('gx', 'gz'), down)]
    all_to_all x0 -> x4, blocking collectives: none -> 91.8 us  [the longest x1 37 us: on_device(): got = lax.all_to_all(sent, ('gx', 'gy'), 0, 0)]
    slice x42 -> x0, local copies, waits for them, and re-layouts: 41.4 us -> none  [the longest x20 24.3 us: padded_2(): first = lax.slice_in_dim(array, 0, width, axis=dim)]
    ppermute x66 -> x2, waiting for transfers between devices: 47 us -> 12.7 us  [the longest x1 7.12 us: on_device(): from_above = lax.ppermute(low, ('gx', 'gz'), down)]
    ppermute x20 -> x0, local copies, waits for them, and re-layouts: 31.3 us -> none  [the longest x10 16.9 us: padded_2(): after = lax.ppermute(first, axis, down)]
    pallas_call x0 -> x6, Pallas kernels: none -> 22.6 us  [the longest x1 13.6 us: on_device(): call(core_kernel, [(1024, 128)], scratch, smem=1, inputs=5)]
  transfers between devices with their start and end apart: 66 -> 2, of which waited for: 38 -> 2; matrix products, arithmetic and copies ran while one was open for 2% -> 0% of each run, Pallas kernels for 0% -> 0%
where the time goes in v1:
time: 139 us; the launch traced here: 138 us
  blocking collectives  91.8 us (66%)
  Pallas kernels  22.6 us (16%)
  waiting for transfers between devices  12.7 us (9%)
  starting transfers between devices  7.06 us (5%)
  local copies, waits for them, and re-layouts  3.31 us (2%)
    all_to_all x1, blocking collectives, on_device(): got = lax.all_to_all(sent, ('gx', 'gy'), 0, 0)  37 us
    all_to_all x1, blocking collectives, on_device(): back = lax.all_to_all(images.reshape(32, 32, 128), ('gx', 'gy'), 0, 0)  21.3 us
    all_to_all x1, blocking collectives, on_device(): gram = lax.all_to_all(gram, 'gz', 0, 0)  18 us
    all_to_all x1, blocking collectives, on_device(): gram = lax.all_to_all(gram, ('gx', 'gy'), 0, 0)  15.5 us
    pallas_call x1, Pallas kernels, on_device(): call(core_kernel, [(1024, 128)], scratch, smem=1, inputs=5)  13.6 us
    ppermute x1, waiting for transfers between devices, on_device(): from_above = lax.ppermute(low, ('gx', 'gz'), down)  7.12 us
    ppermute x1, waiting for transfers between devices, on_device(): from_below = lax.ppermute(high, ('gx', 'gz'), up)  5.57 us
    pallas_call x1, Pallas kernels, on_device(): call(arrange_kernel, [plane, plane, (WIN, 4, 8, 128), msg, msg])  4.6 us
  transfers between devices with their start and end apart: 2, of which 2 were waited for; matrix products, arithmetic and copies ran while one was open for 0% of the time, Pallas kernels for 0%

profile of v1, /device:TPU:1, one launch (start us, length us, event | category | flops | bytes accessed | tf_op | source)
XLA Modules:
  0.0 138.1 jit_solution(6584413037911013982)
XLA Ops:
  0.6 0.0 copy-start
  0.6 1.0 copy-done
  1.7 0.0 copy-start.1
  1.7 0.8 copy-done.1
  2.4 0.0 copy-start.2
  2.4 0.8 copy-done.2
  3.2 0.0 copy-start.3
  3.2 0.8 copy-done.3
  3.9 0.3 shard_map.59
  4.3 37.0 %all_to_all.20 = f32[32,56,128]{2,1,0:T(8,128)S(1)} all-to-all(f32[32,56,128]{2,1,0:T(8,128)S(1)} %shard_map.59), channel_id=1, replica_groups=mesh['gx'=8,'gy'=4,'gz'=16] {'gx','gy'}, dimensions={0} | all-to-all | bytes 1835008 | tf_op jit(solution)/shard_map/all_to_all | solution.py:449
  41.2 4.6 %shard_map.60 = (f32[16,8,8,128]{3,2,1,0:T(8,128)S(1)}, f32[16,8,8,128]{3,2,1,0:T(8,128)S(1)}, f32[16,4,8,128]{3,2,1,0:T(8,128)S(1)}, f32[140,8,128]{2,1,0:T(8,128)S(1)}, f32[140,8,128]{2,1,0:T(8,128)}) custom-call(f32[1792,128]{1,0:T(8,128)S(1)} %bitcast.9), custom_call_target="tpu_custom_call" | custom-call | tf_op jit(solution)/shard_map/pallas_call | solution.py:451
  45.8 2.5 %collective-permute-start = (f32[140,8,128]{2,1,0:T(8,128)}, f32[140,8,128]{2,1,0:T(8,128)S(1)}, u32[]{:S(2)}, u32[]{:S(2)}) collective-permute-start(f32[140,8,128]{2,1,0:T(8,128)} %get-tuple-element.11), channel_id=1, source_target_pairs={{0,64},{64,128},{128,192},{192,256},{256,320},{320,384},{384,448},... | collective-permute-start | bytes 1720328 | tf_op jit(solution)/shard_map/ppermute | solution.py:463
  48.4 4.5 %collective-permute-start.1 = (f32[140,8,128]{2,1,0:T(8,128)S(1)}, f32[140,8,128]{2,1,0:T(8,128)S(1)}, u32[]{:S(2)}, u32[]{:S(2)}) collective-permute-start(f32[140,8,128]{2,1,0:T(8,128)S(1)} %get-tuple-element.15), channel_id=1, source_target_pairs={{64,0},{128,64},{192,128},{256,192},{320,256},{384,320},{448,384},... | collective-permute-start | bytes 1720328 | tf_op jit(solution)/shard_map/ppermute | solution.py:464
  52.9 0.1 add_convert_fusion.edge_ref
  53.0 5.6 %collective-permute-done.lo_ref = f32[140,8,128]{2,1,0:T(8,128)S(1)} collective-permute-done((f32[140,8,128]{2,1,0:T(8,128)}, f32[140,8,128]{2,1,0:T(8,128)S(1)}, u32[]{:S(2)}, u32[]{:S(2)}) %collective-permute-start) | collective-permute-done | bytes 573472 | tf_op jit(solution)/shard_map/ppermute | solution.py:463
  58.6 7.1 %collective-permute-done.1.hi_ref = f32[140,8,128]{2,1,0:T(8,128)S(1)} collective-permute-done((f32[140,8,128]{2,1,0:T(8,128)S(1)}, f32[140,8,128]{2,1,0:T(8,128)S(1)}, u32[]{:S(2)}, u32[]{:S(2)}) %collective-permute-start.1) | collective-permute-done | bytes 573472 | tf_op jit(solution)/shard_map/ppermute | solution.py:464
  65.7 13.6 %shard_map.61 = f32[1024,128]{1,0:T(8,128)S(1)} custom-call(s32[2]{0:T(128)S(1)} %add_convert_fusion.edge_ref, f32[140,8,128]{2,1,0:T(8,128)S(1)} %collective-permute-done.lo_ref, f32[16,8,8,128]{3,2,1,0:T(8,128)S(1)} %get-tuple-element.12.s_own_ref, f32[16,8,8,128]{3,2,1,0:T(8,128)S(1)} %get-tuple-element.13.c_own_ref, ...), custom_call_target="tpu_custom_call" | custom-call | tf_op jit(solution)/shard_map/pallas_call | solution.py:471
  79.3 21.3 %all_to_all.21.in_ref = f32[32,32,128]{2,1,0:T(8,128)S(1)} all-to-all(f32[32,32,128]{2,1,0:T(8,128)S(1)} %bitcast.10), channel_id=1, replica_groups=mesh['gx'=8,'gy'=4,'gz'=16] {'gx','gy'}, dimensions={0} | all-to-all | bytes 1048576 | tf_op jit(solution)/shard_map/all_to_all | solution.py:474
  100.7 0.8 shard_map.62
  101.5 15.5 %all_to_all.22.in_ref = f32[32,8,128]{2,1,0:T(8,128)S(1)} all-to-all(f32[32,8,128]{2,1,0:T(8,128)S(1)} %get-tuple-element.16), channel_id=1, replica_groups=mesh['gx'=8,'gy'=4,'gz'=16] {'gx','gy'}, dimensions={0} | all-to-all | bytes 262144 | tf_op jit(solution)/shard_map/all_to_all | solution.py:476
  117.0 18.0 %all_to_all.23.gram_ref = f32[16,8,128]{2,1,0:T(8,128)S(1)} all-to-all(f32[16,8,128]{2,1,0:T(8,128)S(1)} %shard_map.63), channel_id=1, replica_groups=mesh['gx'=8,'gy'=4,'gz'=16] {'gz'}, dimensions={0} | all-to-all | bytes 131072 | tf_op jit(solution)/shard_map/all_to_all | solution.py:478
  135.0 3.2 %shard_map.64 = (f32[16,64,128]{2,1,0:T(8,128)}, f32[16,16]{1,0:T(8,128)}) custom-call(f32[16,8,128]{2,1,0:T(8,128)S(1)} %all_to_all.23.gram_ref, f32[16,64,128]{2,1,0:T(8,128)S(1)} %get-tuple-element.17.img_ref), custom_call_target="tpu_custom_call" | custom-call | tf_op jit(solution)/shard_map/pallas_call | solution.py:479
  (1 shorter events, 0.0 us)
Async XLA Ops:
  0.6 1.0 copy-start
  1.7 0.8 copy-start.1
  2.4 0.8 copy-start.2
  3.2 0.8 copy-start.3
  45.8 12.7 %collective-permute-start = (f32[140,8,128]{2,1,0:T(8,128)}, f32[140,8,128]{2,1,0:T(8,128)S(1)}, u32[]{:S(2)}, u32[]{:S(2)}) collective-permute-start(f32[140,8,128]{2,1,0:T(8,128)} %get-tuple-element.11), channel_id=1, source_target_pairs={{0,64},{64,128},{128,192},{192,256},{256,320},{320,384},{384,448},... | collective-permute-start | bytes 1720328 | tf_op jit(solution)/shard_map/ppermute | solution.py:463
  48.4 17.3 %collective-permute-start.1 = (f32[140,8,128]{2,1,0:T(8,128)S(1)}, f32[140,8,128]{2,1,0:T(8,128)S(1)}, u32[]{:S(2)}, u32[]{:S(2)}) collective-permute-start(f32[140,8,128]{2,1,0:T(8,128)S(1)} %get-tuple-element.15), channel_id=1, source_target_pairs={{64,0},{128,64},{192,128},{256,192},{320,256},{384,320},{448,384},... | collective-permute-start | bytes 1720328 | tf_op jit(solution)/shard_map/ppermute | solution.py:464

commit v2 on v1

v2 whole, which is shorter than its diff:
```python
import jax
import jax.numpy as jnp
from jax import lax
from jax.experimental import pallas as pl
from jax.experimental.pallas import tpu as pltpu
from jax.sharding import PartitionSpec as P

DEG = 4
SHIFT = 0.5
LOWER = 0.5
UPPER = 33.5
MID = (UPPER + LOWER) / 2.0
HALF = (UPPER - LOWER) / 2.0
RATIO = MID / HALF

PROBES = 16
CELLS = 32 * 64 * 2048
WIN = 16
HALO = 2 * DEG + 2
INNER = DEG + 1
ROWS = WIN + 2 * HALO
UNROLL = 8
MSG = 12 * HALO + 4 * INNER
F32 = jnp.float32

PATHS = (
    ((0, 0), (0, 1), (1, 1), (1, 2), (0, 2), (0, 3), (1, 3), (1, 0)),
    ((1, 0), (1, 1), (2, 1), (2, 2), (1, 2), (1, 3), (2, 3), (2, 0)),
)


def place(block, w, q):
    core, layer = block % 2, block // 2
    gx = (PATHS[core][w][0] + 2 * (q + layer)) % 8
    return gx, PATHS[core][w][1]


def placer():
    block = lax.axis_index("gz")
    core, layer = block % 2, block // 2

    def number(w, q):
        (x0, y0), (x1, y1) = PATHS[0][w], PATHS[1][w]
        gx = (x0 + core * (x1 - x0) + 2 * (q + layer)) % 8
        return gx * 4 + y0 + core * (y1 - y0)

    return number


def lane_sub():
    lane = lax.broadcasted_iota(jnp.int32, (8, 128), 1)
    return lane, lax.broadcasted_iota(jnp.int32, (8, 128), 0)


def swap_groups(v):
    last = v[0].ndim - 1
    lane = lax.broadcasted_iota(jnp.int32, v[0].shape, last)
    high, low = (lane & 64) == 0, (lane & 32) == 0
    u = [None] * 4
    for a in range(2):
        moved = pltpu.roll(jnp.where(high, v[a + 2], v[a]), 64, last)
        u[a] = jnp.where(high, v[a], moved)
        u[a + 2] = jnp.where(high, moved, v[a + 2])
    out = [None] * 4
    for a in (0, 2):
        out[a] = jnp.where(low, u[a], pltpu.roll(u[a + 1], 32, last))
        out[a + 1] = jnp.where(low, pltpu.roll(u[a], 96, last), u[a + 1])
    return out


def pack_kernel(lp_hbm, pr_hbm, dw_hbm, v_hbm, out_ref, lp_ref, pr_ref, dw_ref, v_ref, perm_ref, mix_ref, sems):
    pairs = ((lp_hbm, lp_ref), (v_hbm, v_ref), (pr_hbm, pr_ref), (dw_hbm, dw_ref))
    copies = [pltpu.make_async_copy(a, b, sems.at[i]) for i, (a, b) in enumerate(pairs)]
    for copy in copies:
        copy.start()
    for copy in copies:
        copy.wait()
    perm_ref[...] = jnp.exp(lp_ref[...])
    first = (lane_sub()[0] & 2) == 0
    number = placer()
    dest = [[number(w, q) for q in range(4)] for w in range(8)]

    def mixed(parts):
        for slot in range(4):
            mix_ref[pl.ds(slot, 32, stride=4), :] = parts[slot]
        return mix_ref[...].T

    def half(ref, yl):
        return ref[pl.ds(yl, 32, stride=2), :]

    def paired(tile, w):
        return jnp.where(first, tile[16 * w : 16 * w + 8], tile[16 * w + 8 : 16 * w + 16])

    for yl in range(2):
        perm = half(perm_ref, yl)
        for q in range(4):
            tile = mixed([perm * v_ref[4 * q + p, pl.ds(yl, 32, stride=2), :] for p in range(4)])
            for w in range(8):
                out_ref[dest[w][q], 16 * yl : 16 * yl + 16] = tile[16 * w : 16 * w + 16]
        tile = mixed([perm, half(pr_ref, yl)] * 2)
        for w in range(8):
            packed = paired(tile, w)
            for q in range(4):
                out_ref[dest[w][q], 32 + 8 * yl : 40 + 8 * yl] = packed
    tile = mixed([half(dw_ref, 0), half(dw_ref, 1)] * 2)
    for w in range(8):
        packed = paired(tile, w)
        for q in range(4):
            out_ref[dest[w][q], 48:56] = packed


def widen(v, first):
    last = v.ndim - 1
    return jnp.where(first, v, pltpu.roll(v, 2, last)), jnp.where(first, pltpu.roll(v, 126, last), v)


def split(v, even):
    last = v.ndim - 1
    return jnp.where(even, v, pltpu.roll(v, 1, last)), jnp.where(even, pltpu.roll(v, 127, last), v)


def arrange_kernel(in_ref, s_ref, c_ref, w_ref, low_ref, high_ref):
    first = (lane_sub()[0] & 2) == 0

    def fetch(begin, count):
        got = [
            jnp.stack([in_ref[pl.ds(56 * g + begin + k, 8, stride=224), :] for k in range(count)])
            for g in range(4)
        ]
        return swap_groups(got)

    lift, pairs = WIN - HALO, HALO // 2
    for yl in range(2):
        for begin in range(0, WIN, 8):
            for x, v in enumerate(fetch(16 * yl + begin, 8)):
                n = 4 * yl + x
                s_ref[n, begin : begin + 8] = v
                for k in range(8):
                    z = begin + k
                    if z < HALO:
                        low_ref[HALO * n + z] = v[k]
                    if z >= lift:
                        high_ref[HALO * n + z - lift] = v[k]
        for x, v in enumerate(fetch(32 + 8 * yl, 8)):
            n = 4 * yl + x
            below, above = widen(v, first)
            c_ref[n, 0:8] = below
            c_ref[n, 8:16] = above
            c = [below[z] if z < 8 else above[z - 8] for z in range(WIN)]
            for k in range(pairs):
                at = 8 * HALO + pairs * n + k
                low_ref[at] = jnp.where(first, c[k], c[k + pairs])
                high_ref[at] = jnp.where(first, c[lift + k], c[lift + k + pairs])
    for x, v in enumerate(fetch(48, 8)):
        below, above = widen(v, first)
        w_ref[x, 0:8] = below
        w_ref[x, 8:16] = above
        at = 12 * HALO + INNER * x
        low_ref[at : at + INNER] = below[:INNER]
        high_ref[at : at + INNER] = above[8 - INNER :]


def core_kernel(
    edge_ref, lo_ref, s_own_ref, c_own_ref, w_own_ref, hi_ref, out_ref,
    kx_ref, ky_ref, kz_ref, kd_ref, diag_ref, dx_ref, dy_ref, dz_ref, dd_ref, pd_ref,
    perm_ref, press_ref, wt_ref, s_ref, r_ref, e0_ref, e1_ref, z_ref,
):
    lane, sub = lane_sub()
    first, even = (lane & 2) == 0, (lane & 1) == 0
    at_first, at_last = edge_ref[0].astype(F32), edge_ref[1].astype(F32)

    for n in range(8):
        s_ref[n, HALO : HALO + WIN] = s_own_ref[n]
        perm, press = split(c_own_ref[n], even)
        perm_ref[n, HALO : HALO + WIN] = perm
        press_ref[n, HALO : HALO + WIN] = press
    for x in range(4):
        low, high = split(w_own_ref[x], even)
        wt_ref[x, INNER : INNER + WIN] = low
        wt_ref[4 + x, INNER : INNER + WIN] = high
    pairs = HALO // 2
    for src_ref, base, inner in ((lo_ref, 0, 0), (hi_ref, HALO + WIN, INNER + WIN)):
        for n in range(8):
            begin = HALO * n
            s_ref[n, base : base + HALO] = src_ref[begin : begin + HALO]
            begin = 8 * HALO + pairs * n
            for part, c in enumerate(widen(src_ref[begin : begin + pairs], first)):
                at = base + pairs * part
                perm, press = split(c, even)
                perm_ref[n, at : at + pairs] = perm
                press_ref[n, at : at + pairs] = press
        for x in range(4):
            begin = 12 * HALO + INNER * x
            low, high = split(src_ref[begin : begin + INNER], even)
            wt_ref[x, inner : inner + INNER] = low
            wt_ref[4 + x, inner : inner + INNER] = high

    def mark(n):
        none = jnp.zeros((8, 128), F32)
        return (
            jnp.where(sub == 0, 0.5, 0.0) if n % 4 == 0 else none,
            jnp.where(sub == 7, 0.5, 0.0) if n % 4 == 3 else none,
            jnp.where(lane < 4, 0.5, 0.0) if n < 4 else none,
            jnp.where(lane >= 124, 0.5, 0.0) if n >= 4 else none,
        )

    ends = [mark(n) for n in range(8)]

    def far(v):
        return (
            [pltpu.roll(v[n], 7, 1) for n in (0, 4)]
            + [pltpu.roll(v[n], 1, 1) for n in (3, 7)]
            + [pltpu.roll(v[n], 124, 2) for n in range(4)]
            + [pltpu.roll(v[n + 4], 4, 2) for n in range(4)]
        )

    def coefficients(step, carry):
        here, above = pl.ds(5 * step, 5), pl.ds(5 * step + 1, 5)
        perm = [perm_ref[n, here] for n in range(8)]
        press = [press_ref[n, here] for n in range(8)]
        perm_far, press_far = far(perm), far(press)
        outs = []
        for n in range(8):
            x_begin, x_end, y_begin, y_end = ends[n]
            outside = (x_begin + x_end) + (y_begin + y_end)
            half_x, half_y = 0.5 - x_end, 0.5 - y_end
            near = (n + 1, None) if n % 4 < 3 else (None, n // 4)
            for field, field_far, out_ref, sign in (
                (perm, perm_far, kx_ref, 1.0),
                (press, press_far, dx_ref, -1.0),
            ):
                up = field_far[near[1]] if near[0] is None else field[near[0]]
                outs.append((out_ref, n, half_x * (field[n] + sign * up)))
            for field, field_far, out_ref, sign in (
                (perm, perm_far, ky_ref, 1.0),
                (press, press_far, dy_ref, -1.0),
            ):
                up = field[n + 4] if n < 4 else field_far[n]
                outs.append((out_ref, n, half_y * (field[n] + sign * up)))
            outs.append((kz_ref, n, 0.5 * (perm[n] + perm_ref[n, above])))
            outs.append((dz_ref, n, 0.5 * (press[n] - press_ref[n, above])))
            outs.append((diag_ref, n, SHIFT + outside * perm[n]))
            outs.append((pd_ref, n, outside * press[n]))
        for i, n in enumerate((0, 4, 0, 1, 2, 3)):
            half = 0.5 - ends[n][0 if i < 2 else 2]
            at = 2 + i if i < 2 else 6 + i
            outs.append((kd_ref, i, half * (perm[n] + perm_far[at])))
            outs.append((dd_ref, i, half * (press_far[at] - press[n])))
        for ref, n, value in outs:
            ref[n, here] = value
        return carry

    lax.fori_loop(0, (ROWS - 1) // 5, coefficients, 0)
    for row, inside, end in ((HALO - 1, HALO, at_first), (HALO + WIN - 1, HALO + WIN - 1, at_last)):
        for n in range(8):
            kz_ref[n, row] = kz_ref[n, row] * (1.0 - end)
            dz_ref[n, row] = dz_ref[n, row] * (1.0 - end)
            diag_ref[n, inside] = diag_ref[n, inside] + (0.5 * end) * perm_ref[n, inside]
            pd_ref[n, inside] = pd_ref[n, inside] + (0.5 * end) * press_ref[n, inside]

    def sweep(field_ref, begin, end, face_refs, centre_ref, join, sign, inputs, finish):
        fx_ref, fy_ref, fz_ref, fd_ref = face_refs

        def part(up, down):
            return up - down if sign < 0 else up + down

        def rows(row, count):
            here, below = pl.ds(row, count), pl.ds(row - 1, count + 1)
            now = [field_ref[n, here] for n in range(8)]
            around = far(now)
            flow_x, back_x, flow_y, back_y = ([None] * 8 for _ in range(4))
            for n in range(8):
                up = now[n + 1] if n % 4 < 3 else around[n // 4]
                flow_x[n] = join(now[n], up) * fx_ref[n, here]
                up = now[n + 4] if n < 4 else around[n]
                flow_y[n] = join(now[n], up) * fy_ref[n, here]
            for n in range(8):
                if n % 4:
                    back_x[n] = flow_x[n - 1]
                else:
                    back_x[n] = join(around[2 + n // 4], now[n]) * fd_ref[n // 4, here]
                if n >= 4:
                    back_y[n] = flow_y[n - 4]
                else:
                    back_y[n] = join(around[8 + n], now[n]) * fd_ref[2 + n, here]
            results = []
            for n in range(8):
                flow_z = join(field_ref[n, below], field_ref[n, pl.ds(row, count + 1)])
                flow_z = flow_z * fz_ref[n, below]
                total = centre_ref[n, here] * now[n] + part(flow_x[n], back_x[n])
                total = total + (part(flow_y[n], back_y[n]) + part(flow_z[1:], flow_z[:-1]))
                extra = [ref[n, here] for ref in inputs]
                results.append((n, finish(row, count, n, now[n], total, *extra)))
            for n, outs in results:
                for ref, value in outs:
                    ref[n, here] = value

        steps, rest = divmod(end - begin, UNROLL)

        def body(i, carry):
            rows(begin + UNROLL * i, UNROLL)
            return carry

        lax.fori_loop(0, steps, body, 0)
        if rest:
            rows(end - rest, rest)

    def add(a, b):
        return a + b

    def minus(a, b):
        return a - b

    def start(value):
        direction = value * (1.0 / MID)
        return [(r_ref, value), (e0_ref, direction), (z_ref, direction)]

    def solve(lowest, finish_last):
        weight_now = 1.0 / RATIO
        here, there = e0_ref, e1_ref
        for repeat in range(DEG):
            weight_next = 1.0 / (2.0 * RATIO - weight_now)
            keep, take = weight_next * weight_now, 2.0 * weight_next / HALF
            weight_now = weight_next
            last = repeat == DEG - 1

            def finish(row, count, n, v, total, residual, iterate, k=keep, m=take, to=there, last=last):
                residual = residual - total
                direction = k * v + m * residual
                iterate = iterate + direction
                if last:
                    return finish_last(row, count, n, iterate)
                return [(r_ref, residual), (to, direction), (z_ref, iterate)]

            begin = lowest + 1 + repeat
            faces = (kx_ref, ky_ref, kz_ref, kd_ref)
            sweep(here, begin, ROWS - begin, faces, diag_ref, minus, -1, (r_ref, z_ref), finish)
            here, there = there, here

    faces = (dx_ref, dy_ref, dz_ref, dd_ref)
    sweep(
        s_ref, 1, ROWS - 1, faces, pd_ref, add, -1, (), lambda row, count, n, v, total: start(total)
    )
    skip = HALO - INNER

    def second(row, count, n, value):
        return start(value * wt_ref[n, pl.ds(row - skip, count)])

    solve(1, second)
    solve(skip, lambda row, count, n, value: [(s_ref, value)])

    def image(row, count, n, v, total):
        return [(z_ref, perm_ref[n, pl.ds(row, count)] * total)]

    sweep(s_ref, HALO, HALO + WIN, faces, pd_ref, minus, 1, (), image)

    for yl in range(2):
        for begin in range(0, WIN, 8):
            at = slice(HALO + begin, HALO + begin + 8)
            v = swap_groups([z_ref[4 * yl + x, at] for x in range(4)])
            for g in range(4):
                for k in range(8):
                    to = g * 2 * WIN + yl * WIN + begin + k
                    out_ref[pl.ds(to, 8, stride=8 * WIN), :] = v[g][k]


def gram_kernel(in_ref, img_ref, gram_ref, acc_ref, mix_ref):
    number = placer()
    for q in range(4):
        source = [number(w, q) for w in range(8)]
        for yl in range(2):
            rows = [in_ref[source[w], 16 * yl : 16 * yl + 16] for w in range(8)]
            mix_ref[yl] = jnp.concatenate(rows, axis=0).T
            for p in range(4):
                img_ref[4 * q + p, pl.ds(yl, 32, stride=2), :] = mix_ref[
                    yl, pl.ds(p, 32, stride=4), :
                ]
    for i in range(PROBES):
        a = [img_ref[i, 8 * k : 8 * k + 8] for k in range(8)]
        for j in range(i + 1):
            parts = [a[k] * img_ref[j, 8 * k : 8 * k + 8] for k in range(8)]
            while len(parts) > 1:
                parts = [parts[k] + parts[k + 1] for k in range(0, len(parts), 2)]
            begin = (16 * i + j) * 8
            acc_ref[begin : begin + 8] = parts[0]
            begin = (16 * j + i) * 8
            acc_ref[begin : begin + 8] = parts[0]
    sums = []
    for c in range(32):
        parts = [acc_ref[pl.ds(64 * c + s, 8, stride=8), :] for s in range(8)]
        while len(parts) > 1:
            parts = [parts[k] + parts[k + 1] for k in range(0, len(parts), 2)]
        sums.append(parts[0])
    total = lax.dot_general(
        jnp.ones((8, 128), F32),
        jnp.concatenate(sums, axis=0),
        (((1,), (1,)), ((), ())),
        precision=lax.Precision.HIGHEST,
        preferred_element_type=F32,
    )
    _, sub = lane_sub()
    tile = jnp.where(sub == 0, total[:, :128], total[:, 128:])
    for d in range(32):
        gram_ref[d] = tile[0:2]


def spread_kernel(in_ref, out_ref):
    total = jnp.sum(in_ref[...], axis=0)
    for d in range(16):
        out_ref[d] = total


def finish_kernel(gram_ref, img_ref, out_ref, factor_ref, inv_ref):
    total = jnp.sum(gram_ref[...], axis=0) * (1.0 / CELLS)
    lane = lax.broadcasted_iota(jnp.int32, (16, 128), 1)
    row = lax.broadcasted_iota(jnp.int32, (16, 128), 0)
    g = jnp.concatenate(
        [jnp.broadcast_to(total[0:1], (8, 128)), jnp.broadcast_to(total[1:2], (8, 128))], axis=0
    )
    g = jnp.where((lane >> 4) == (row & 7), g, 0.0)
    for step in (16, 32, 64):
        g = g + pltpu.roll(g, step, 1)
    g = jnp.where(lane < 16, g, jnp.where(lane == row + 16, 1.0, 0.0))
    for k in range(PROBES - 1):
        pivot_row = jnp.broadcast_to(g[k : k + 1], (16, 128))
        column = jnp.broadcast_to(g[:, k : k + 1], (16, 128))
        pivot = jnp.broadcast_to(pivot_row[:, k : k + 1], (16, 128))
        g = g - jnp.where(row > k, column / pivot, 0.0) * pivot_row
    diagonal = jnp.sum(jnp.where(lane == row, g, 0.0), axis=1, keepdims=True)
    g = g / jnp.sqrt(diagonal)
    factor_ref[...] = jnp.where(lane >= row, g, 0.0)[:, :16]
    for j in range(PROBES):
        inv_ref[j] = jnp.broadcast_to(g[:, 16 + j : 17 + j], (16, 128))
    for i in range(PROBES):
        value = jnp.broadcast_to(inv_ref[0, i : i + 1], (64, 128)) * img_ref[0]
        for j in range(1, i + 1):
            value = value + jnp.broadcast_to(inv_ref[j, i : i + 1], (64, 128)) * img_ref[j]
        out_ref[i] = value


def call(kernel, out_shapes, scratch=(), smem=0, inputs=1, copies=0):
    out_shape = [jax.ShapeDtypeStruct(s, F32) for s in out_shapes]
    vmem = pl.BlockSpec(memory_space=pltpu.VMEM)
    given = pl.BlockSpec(memory_space=pltpu.HBM) if copies else vmem
    specs = [pl.BlockSpec(memory_space=pltpu.SMEM)] * smem + [given] * inputs
    sems = [pltpu.SemaphoreType.DMA((copies,))] if copies else []
    return pl.pallas_call(
        kernel,
        out_shape=out_shape,
        in_specs=specs,
        out_specs=[vmem] * len(out_shape),
        scratch_shapes=[pltpu.VMEM(s, F32) for s in scratch] + sems,
        compiler_params=pltpu.CompilerParams(vmem_limit_bytes=40 * 1024 * 1024),
    )


def on_device(log_perm, pressure, data_weight, probes):
    planes = [a.reshape(64, 128) for a in (log_perm, pressure, data_weight)]
    block = (64, 128)
    scratch = [block, block, block, (16, 64, 128), block, (128, 128)]
    (sent,) = call(pack_kernel, [(32, 56, 128)], scratch, inputs=4, copies=4)(
        *planes, probes.reshape(16, 64, 128)
    )
    got = lax.all_to_all(sent, ("gx", "gy"), 0, 0)
    plane, msg = (8, WIN, 8, 128), (MSG, 8, 128)
    own_s, own_c, own_w, low, high = call(
        arrange_kernel, [plane, plane, (4, WIN, 8, 128), msg, msg]
    )(got.reshape(32 * 56, 128))

    blocks = lax.axis_size("gz")
    up = []
    for q in range(4):
        route = []
        for n in range(8 * blocks):
            gx, gy = place(n // 8, n % 8, q)
            route.append((gx * 4 + gy) * blocks + n // 8)
        up += [(route[n], route[n + 1]) for n in range(len(route) - 1)]
    down = [(j, i) for i, j in up]
    from_below = lax.ppermute(high, ("gx", "gy", "gz"), up)
    from_above = lax.ppermute(low, ("gx", "gy", "gz"), down)
    block = lax.axis_index("gz")
    at_end = (lax.axis_index("gx") % 2 == 0) & (lax.axis_index("gy") == 0)
    edge = jnp.stack([at_end & (block == 0), at_end & (block == blocks - 1)]).astype(jnp.int32)
    field = (8, ROWS, 8, 128)
    far = (6, ROWS, 8, 128)
    scratch = ([field] * 3 + [far, field]) * 2
    scratch += [field] * 2 + [(8, WIN + 2 * INNER, 8, 128)] + [field] * 5
    (images,) = call(core_kernel, [(1024, 128)], scratch, smem=1, inputs=5)(
        edge, from_below, own_s, own_c, own_w, from_above
    )
    back = lax.all_to_all(images.reshape(32, 32, 128), ("gx", "gy"), 0, 0)
    image_rows, gram = call(
        gram_kernel, [(16, 64, 128), (32, 2, 128)], [(2048, 128), (2, 128, 128)]
    )(back)
    gram = lax.all_to_all(gram, ("gx", "gy"), 0, 0)
    (gram,) = call(spread_kernel, [(16, 2, 128)])(gram)
    gram = lax.all_to_all(gram, "gz", 0, 0)
    basis, factor = call(
        finish_kernel, [(16, 64, 128), (16, 16)], [(16, 16, 128)], inputs=2
    )(gram, image_rows)
    return (basis.reshape(probes.shape), factor)


def solution(mesh):
    in_specs = (
        P("gx", "gy", "gz"),
        P("gx", "gy", "gz"),
        P("gx", "gy", "gz"),
        P(None, "gx", "gy", "gz"),
    )
    out_specs = (P(None, "gx", "gy", "gz"), P())
    return jax.shard_map(
        on_device, mesh=mesh, in_specs=in_specs, out_specs=out_specs, check_vma=False
    )
```

time: 139 us -> 127 us (0.914)
  Pallas kernels: 22.6 us -> 17.4 us
  blocking collectives: 91.8 us -> 87.9 us
  waiting for transfers between devices: 12.7 us -> 9.29 us
    all_to_all x1, blocking collectives: 21.3 us -> 17.9 us  [on_device(): back = lax.all_to_all(images.reshape(32, 32, 128), ('gx', 'gy'), 0, 0)]
    ppermute x2, waiting for transfers between devices: 12.7 us -> 9.29 us  [the longest x1 4.92 us: on_device(): from_below = lax.ppermute(high, ('gx', 'gy', 'gz'), up)]
    pallas_call x1, Pallas kernels: 13.6 us -> 10.8 us  [on_device(): call(core_kernel, [(1024, 128)], scratch, smem=1, inputs=5)]
    pallas_call x4, Pallas kernels: 5.78 us -> 3.39 us  [the longest x1 2.05 us: on_device(): call(arrange_kernel, [plane, plane, (4, WIN, 8, 128), msg, msg])]
where the time goes in v2:
time: 127 us
  blocking collectives  87.9 us (69%)
  Pallas kernels  17.4 us (14%)
  waiting for transfers between devices  9.29 us (7%)
  starting transfers between devices  8.1 us (6%)
  local copies, waits for them, and re-layouts  3.31 us (3%)
    all_to_all x1, blocking collectives, on_device(): got = lax.all_to_all(sent, ('gx', 'gy'), 0, 0)  37 us
    all_to_all x1, blocking collectives, on_device(): gram = lax.all_to_all(gram, 'gz', 0, 0)  18.4 us
    all_to_all x1, blocking collectives, on_device(): back = lax.all_to_all(images.reshape(32, 32, 128), ('gx', 'gy'), 0, 0)  17.9 us
    all_to_all x1, blocking collectives, on_device(): gram = lax.all_to_all(gram, ('gx', 'gy'), 0, 0)  14.6 us
    pallas_call x1, Pallas kernels, on_device(): call(core_kernel, [(1024, 128)], scratch, smem=1, inputs=5)  10.8 us
    ppermute x1, starting transfers between devices, on_device(): from_below = lax.ppermute(high, ('gx', 'gy', 'gz'), up)  6.18 us
    ppermute x1, waiting for transfers between devices, on_device(): from_below = lax.ppermute(high, ('gx', 'gy', 'gz'), up)  4.92 us
    ppermute x1, waiting for transfers between devices, on_device(): from_above = lax.ppermute(low, ('gx', 'gy', 'gz'), down)  4.37 us
  transfers between devices with their start and end apart: 2, of which 2 were waited for; matrix products, arithmetic and copies ran while one was open for 0% of the time, Pallas kernels for 0%

profile of v2, /device:TPU:1, one launch (start us, length us, event | category | flops | bytes accessed | tf_op | source)
XLA Modules:
  0.0 126.7 jit_solution(7228359267476969832)
XLA Ops:
  0.6 0.0 copy-start
  0.6 1.0 copy-done
  1.7 0.0 copy-start.1
  1.7 0.8 copy-done.1
  2.4 0.0 copy-start.2
  2.4 0.8 copy-done.2
  3.2 0.0 copy-start.3
  3.2 0.8 copy-done.3
  3.9 0.5 shard_map.59
  4.4 37.0 %all_to_all.20 = f32[32,56,128]{2,1,0:T(8,128)S(1)} all-to-all(f32[32,56,128]{2,1,0:T(8,128)S(1)} %shard_map.59), channel_id=1, replica_groups=mesh['gx'=8,'gy'=4,'gz'=16] {'gx','gy'}, dimensions={0} | all-to-all | bytes 1835008 | tf_op jit(solution)/shard_map/all_to_all | solution.py:464
  41.4 2.1 %shard_map.60 = (f32[8,16,8,128]{3,2,1,0:T(8,128)S(1)}, f32[8,16,8,128]{3,2,1,0:T(8,128)S(1)}, f32[4,16,8,128]{3,2,1,0:T(8,128)S(1)}, f32[140,8,128]{2,1,0:T(8,128)S(1)}, f32[140,8,128]{2,1,0:T(8,128)}) custom-call(f32[1792,128]{1,0:T(8,128)S(1)} %bitcast.9), custom_call_target="tpu_custom_call" | custom-call | tf_op jit(solution)/shard_map/pallas_call | solution.py:466
  43.5 6.2 %collective-permute-start = (f32[140,8,128]{2,1,0:T(8,128)}, f32[140,8,128]{2,1,0:T(8,128)S(1)}, u32[]{:S(2)}, u32[]{:S(2)}) collective-permute-start(f32[140,8,128]{2,1,0:T(8,128)} %get-tuple-element.11), channel_id=1, source_target_pairs={{0,16},{16,80},{80,96},{96,32},{32,48},{48,112},{112,64},{64,65},{... | collective-permute-start | bytes 1720328 | tf_op jit(solution)/shard_map/ppermute | solution.py:479
  49.6 1.9 %collective-permute-start.1 = (f32[140,8,128]{2,1,0:T(8,128)S(1)}, f32[140,8,128]{2,1,0:T(8,128)S(1)}, u32[]{:S(2)}, u32[]{:S(2)}) collective-permute-start(f32[140,8,128]{2,1,0:T(8,128)S(1)} %get-tuple-element.15), channel_id=1, source_target_pairs={{16,0},{80,16},{96,80},{32,96},{48,32},{112,48},{64,112},{65,64},{... | collective-permute-start | bytes 1720328 | tf_op jit(solution)/shard_map/ppermute | solution.py:480
  51.6 0.1 add_convert_fusion.edge_ref
  51.7 4.9 %collective-permute-done.lo_ref = f32[140,8,128]{2,1,0:T(8,128)S(1)} collective-permute-done((f32[140,8,128]{2,1,0:T(8,128)}, f32[140,8,128]{2,1,0:T(8,128)S(1)}, u32[]{:S(2)}, u32[]{:S(2)}) %collective-permute-start) | collective-permute-done | bytes 573472 | tf_op jit(solution)/shard_map/ppermute | solution.py:479
  56.6 4.4 %collective-permute-done.1.hi_ref = f32[140,8,128]{2,1,0:T(8,128)S(1)} collective-permute-done((f32[140,8,128]{2,1,0:T(8,128)S(1)}, f32[140,8,128]{2,1,0:T(8,128)S(1)}, u32[]{:S(2)}, u32[]{:S(2)}) %collective-permute-start.1) | collective-permute-done | bytes 573472 | tf_op jit(solution)/shard_map/ppermute | solution.py:480
  61.0 10.8 %shard_map.61 = f32[1024,128]{1,0:T(8,128)S(1)} custom-call(s32[2]{0:T(128)S(1)} %add_convert_fusion.edge_ref, f32[140,8,128]{2,1,0:T(8,128)S(1)} %collective-permute-done.lo_ref, f32[8,16,8,128]{3,2,1,0:T(8,128)S(1)} %get-tuple-element.12.s_own_ref, f32[8,16,8,128]{3,2,1,0:T(8,128)S(1)} %get-tuple-element.13.c_own_ref, ...), custom_call_target="tpu_custom_call" | custom-call | tf_op jit(solution)/shard_map/pallas_call | solution.py:488
  71.8 17.9 %all_to_all.21.in_ref = f32[32,32,128]{2,1,0:T(8,128)S(1)} all-to-all(f32[32,32,128]{2,1,0:T(8,128)S(1)} %bitcast.10), channel_id=1, replica_groups=mesh['gx'=8,'gy'=4,'gz'=16] {'gx','gy'}, dimensions={0} | all-to-all | bytes 1048576 | tf_op jit(solution)/shard_map/all_to_all | solution.py:491
  89.7 0.8 shard_map.62
  90.5 14.6 %all_to_all.22.in_ref = f32[32,2,128]{2,1,0:T(2,128)S(1)} all-to-all(f32[32,2,128]{2,1,0:T(2,128)S(1)} %get-tuple-element.16), channel_id=1, replica_groups=mesh['gx'=8,'gy'=4,'gz'=16] {'gx','gy'}, dimensions={0} | all-to-all | bytes 65536 | tf_op jit(solution)/shard_map/all_to_all | solution.py:495
  105.1 18.4 %all_to_all.23.gram_ref = f32[16,2,128]{2,1,0:T(2,128)S(1)} all-to-all(f32[16,2,128]{2,1,0:T(2,128)S(1)} %shard_map.63), channel_id=1, replica_groups=mesh['gx'=8,'gy'=4,'gz'=16] {'gz'}, dimensions={0} | all-to-all | bytes 32768 | tf_op jit(solution)/shard_map/all_to_all | solution.py:497
  123.6 3.2 %shard_map.64 = (f32[16,64,128]{2,1,0:T(8,128)}, f32[16,16]{1,0:T(8,128)}) custom-call(f32[16,2,128]{2,1,0:T(2,128)S(1)} %all_to_all.23.gram_ref, f32[16,64,128]{2,1,0:T(8,128)S(1)} %get-tuple-element.17.img_ref), custom_call_target="tpu_custom_call" | custom-call | tf_op jit(solution)/shard_map/pallas_call | solution.py:498
  (1 shorter events, 0.0 us)
Async XLA Ops:
  0.6 1.0 copy-start
  1.7 0.8 copy-start.1
  2.4 0.8 copy-start.2
  3.2 0.8 copy-start.3
  43.5 13.1 %collective-permute-start = (f32[140,8,128]{2,1,0:T(8,128)}, f32[140,8,128]{2,1,0:T(8,128)S(1)}, u32[]{:S(2)}, u32[]{:S(2)}) collective-permute-start(f32[140,8,128]{2,1,0:T(8,128)} %get-tuple-element.11), channel_id=1, source_target_pairs={{0,16},{16,80},{80,96},{96,32},{32,48},{48,112},{112,64},{64,65},{... | collective-permute-start | bytes 1720328 | tf_op jit(solution)/shard_map/ppermute | solution.py:479
  49.6 11.3 %collective-permute-start.1 = (f32[140,8,128]{2,1,0:T(8,128)S(1)}, f32[140,8,128]{2,1,0:T(8,128)S(1)}, u32[]{:S(2)}, u32[]{:S(2)}) collective-permute-start(f32[140,8,128]{2,1,0:T(8,128)S(1)} %get-tuple-element.15), channel_id=1, source_target_pairs={{16,0},{80,16},{96,80},{32,96},{48,32},{112,48},{64,112},{65,64},{... | collective-permute-start | bytes 1720328 | tf_op jit(solution)/shard_map/ppermute | solution.py:480

commit v3 on v2

--- a/solution.py
+++ b/solution.py
@@ -19,7 +19,8 @@
 HALO = 2 * DEG + 2
 INNER = DEG + 1
 ROWS = WIN + 2 * HALO
-UNROLL = 8
+UNROLL = 16
+BLOCK = 7
 MSG = 12 * HALO + 4 * INNER
 F32 = jnp.float32
 
@@ -68,22 +69,23 @@
     return out
 
 
-def pack_kernel(lp_hbm, pr_hbm, dw_hbm, v_hbm, out_ref, lp_ref, pr_ref, dw_ref, v_ref, perm_ref, mix_ref, sems):
-    pairs = ((lp_hbm, lp_ref), (v_hbm, v_ref), (pr_hbm, pr_ref), (dw_hbm, dw_ref))
-    copies = [pltpu.make_async_copy(a, b, sems.at[i]) for i, (a, b) in enumerate(pairs)]
+def pack_kernel(
+    lp_hbm, pr_hbm, dw_hbm, v_hbm, out_hbm,
+    lp_ref, pr_ref, dw_ref, v_ref, perm_ref, mix_ref, out_ref, in_sems, out_sems,
+):
+    pairs = [(lp_hbm, lp_ref), (pr_hbm, pr_ref), (dw_hbm, dw_ref)]
+    pairs += [(v_hbm.at[pl.ds(4 * q, 4)], v_ref.at[pl.ds(4 * q, 4)]) for q in range(4)]
+    copies = [pltpu.make_async_copy(a, b, in_sems.at[i]) for i, (a, b) in enumerate(pairs)]
     for copy in copies:
         copy.start()
-    for copy in copies:
-        copy.wait()
-    perm_ref[...] = jnp.exp(lp_ref[...])
     first = (lane_sub()[0] & 2) == 0
     number = placer()
     dest = [[number(w, q) for q in range(4)] for w in range(8)]
 
-    def mixed(parts):
+    def mixed(parts, at):
         for slot in range(4):
-            mix_ref[pl.ds(slot, 32, stride=4), :] = parts[slot]
-        return mix_ref[...].T
+            mix_ref[at, pl.ds(slot, 32, stride=4), :] = parts[slot]
+        return mix_ref[at].T
 
     def half(ref, yl):
         return ref[pl.ds(yl, 32, stride=2), :]
@@ -91,22 +93,35 @@
     def paired(tile, w):
         return jnp.where(first, tile[16 * w : 16 * w + 8], tile[16 * w + 8 : 16 * w + 16])
 
-    for yl in range(2):
-        perm = half(perm_ref, yl)
-        for q in range(4):
-            tile = mixed([perm * v_ref[4 * q + p, pl.ds(yl, 32, stride=2), :] for p in range(4)])
+    for copy in copies[:3]:
+        copy.wait()
+    perm_ref[...] = jnp.exp(lp_ref[...])
+    perm = [half(perm_ref, yl) for yl in range(2)]
+    tiles = [mixed([perm[yl], half(pr_ref, yl)] * 2, yl) for yl in range(2)]
+    tiles.append(mixed([half(dw_ref, 0), half(dw_ref, 1)] * 2, 2))
+    for w in range(8):
+        for i in range(3):
+            packed = paired(tiles[i], w)
+            for q in range(4):
+                out_ref[dest[w][q], 32 + 8 * i : 40 + 8 * i] = packed
+    sends = []
+    for q in range(4):
+        copies[3 + q].wait()
+        for yl in range(2):
+            fields = [
+                perm[yl] * v_ref[4 * q + p, pl.ds(yl, 32, stride=2), :] for p in range(4)
+            ]
+            tile = mixed(fields, 3 + yl)
             for w in range(8):
                 out_ref[dest[w][q], 16 * yl : 16 * yl + 16] = tile[16 * w : 16 * w + 16]
-        tile = mixed([perm, half(pr_ref, yl)] * 2)
         for w in range(8):
-            packed = paired(tile, w)
-            for q in range(4):
-                out_ref[dest[w][q], 32 + 8 * yl : 40 + 8 * yl] = packed
-    tile = mixed([half(dw_ref, 0), half(dw_ref, 1)] * 2)
-    for w in range(8):
-        packed = paired(tile, w)
-        for q in range(4):
-            out_ref[dest[w][q], 48:56] = packed
+            at = dest[w][q]
+            sends.append(
+                pltpu.make_async_copy(out_ref.at[at], out_hbm.at[at], out_sems.at[8 * q + w])
+            )
+            sends[-1].start()
+    for send in sends:
+        send.wait()
 
 
 def widen(v, first):
@@ -163,8 +178,9 @@
 def core_kernel(
     edge_ref, lo_ref, s_own_ref, c_own_ref, w_own_ref, hi_ref, out_ref,
     kx_ref, ky_ref, kz_ref, kd_ref, diag_ref, dx_ref, dy_ref, dz_ref, dd_ref, pd_ref,
-    perm_ref, press_ref, wt_ref, s_ref, r_ref, e0_ref, e1_ref, z_ref,
+    perm_ref, press_ref, wt_ref, s_ref, *e_refs,
 ):
+    image_ref = e_refs[1]
     lane, sub = lane_sub()
     first, even = (lane & 2) == 0, (lane & 1) == 0
     at_first, at_last = edge_ref[0].astype(F32), edge_ref[1].astype(F32)
@@ -215,7 +231,7 @@
         )
 
     def coefficients(step, carry):
-        here, above = pl.ds(5 * step, 5), pl.ds(5 * step + 1, 5)
+        here, above = pl.ds(BLOCK * step, BLOCK), pl.ds(BLOCK * step + 1, BLOCK)
         perm = [perm_ref[n, here] for n in range(8)]
         press = [press_ref[n, here] for n in range(8)]
         perm_far, press_far = far(perm), far(press)
@@ -250,7 +266,7 @@
             ref[n, here] = value
         return carry
 
-    lax.fori_loop(0, (ROWS - 1) // 5, coefficients, 0)
+    lax.fori_loop(0, (ROWS - 1) // BLOCK, coefficients, 0)
     for row, inside, end in ((HALO - 1, HALO, at_first), (HALO + WIN - 1, HALO + WIN - 1, at_last)):
         for n in range(8):
             kz_ref[n, row] = kz_ref[n, row] * (1.0 - end)
@@ -311,53 +327,57 @@
     def minus(a, b):
         return a - b
 
-    def start(value):
-        direction = value * (1.0 / MID)
-        return [(r_ref, value), (e0_ref, direction), (z_ref, direction)]
-
     def solve(lowest, finish_last):
-        weight_now = 1.0 / RATIO
-        here, there = e0_ref, e1_ref
+        keep_now, take_now, weight_now = 0.0, 1.0 / MID, 1.0 / RATIO
         for repeat in range(DEG):
             weight_next = 1.0 / (2.0 * RATIO - weight_now)
             keep, take = weight_next * weight_now, 2.0 * weight_next / HALF
-            weight_now = weight_next
+            grow, drop = keep + take / take_now, take * keep_now / take_now
+            keep_now, take_now, weight_now = keep, take, weight_next
             last = repeat == DEG - 1
 
-            def finish(row, count, n, v, total, residual, iterate, k=keep, m=take, to=there, last=last):
-                residual = residual - total
-                direction = k * v + m * residual
-                iterate = iterate + direction
-                if last:
-                    return finish_last(row, count, n, iterate)
-                return [(r_ref, residual), (to, direction), (z_ref, iterate)]
-
+            def finish(row, count, n, v, total, *old, grow=grow, drop=drop, take=take, i=repeat):
+                direction = grow * v - take * total
+                if i:
+                    direction = direction - drop * old[0]
+                if i < DEG - 1:
+                    return [(e_refs[i + 1], direction)]
+                iterate = direction + v
+                for e in old:
+                    iterate = iterate + e
+                return finish_last(row, count, n, iterate)
+
+            old = e_refs[repeat - 1 :: -1] if last else e_refs[repeat - 1 : repeat]
             begin = lowest + 1 + repeat
             faces = (kx_ref, ky_ref, kz_ref, kd_ref)
-            sweep(here, begin, ROWS - begin, faces, diag_ref, minus, -1, (r_ref, z_ref), finish)
-            here, there = there, here
+            sweep(
+                e_refs[repeat], begin, ROWS - begin, faces, diag_ref, minus, -1,
+                old if repeat else (), finish,
+            )
 
     faces = (dx_ref, dy_ref, dz_ref, dd_ref)
-    sweep(
-        s_ref, 1, ROWS - 1, faces, pd_ref, add, -1, (), lambda row, count, n, v, total: start(total)
-    )
+
+    def start(row, count, n, v, total):
+        return [(e_refs[0], total * (1.0 / MID))]
+
+    sweep(s_ref, 1, ROWS - 1, faces, pd_ref, add, -1, (), start)
     skip = HALO - INNER
 
     def second(row, count, n, value):
-        return start(value * wt_ref[n, pl.ds(row - skip, count)])
+        return [(e_refs[0], value * (wt_ref[n, pl.ds(row - skip, count)] * (1.0 / MID)))]
 
     solve(1, second)
     solve(skip, lambda row, count, n, value: [(s_ref, value)])
 
     def image(row, count, n, v, total):
-        return [(z_ref, perm_ref[n, pl.ds(row, count)] * total)]
+        return [(image_ref, perm_ref[n, pl.ds(row, count)] * total)]
 
     sweep(s_ref, HALO, HALO + WIN, faces, pd_ref, minus, 1, (), image)
 
     for yl in range(2):
         for begin in range(0, WIN, 8):
             at = slice(HALO + begin, HALO + begin + 8)
-            v = swap_groups([z_ref[4 * yl + x, at] for x in range(4)])
+            v = swap_groups([image_ref[4 * yl + x, at] for x in range(4)])
             for g in range(4):
                 for k in range(8):
                     to = g * 2 * WIN + yl * WIN + begin + k
@@ -410,7 +430,7 @@
         out_ref[d] = total
 
 
-def finish_kernel(gram_ref, img_ref, out_ref, factor_ref, inv_ref):
+def finish_kernel(gram_ref, img_ref, out_hbm, factor_ref, inv_ref, out_ref, sems):
     total = jnp.sum(gram_ref[...], axis=0) * (1.0 / CELLS)
     lane = lax.broadcasted_iota(jnp.int32, (16, 128), 1)
     row = lax.broadcasted_iota(jnp.int32, (16, 128), 0)
@@ -420,45 +440,55 @@
     g = jnp.where((lane >> 4) == (row & 7), g, 0.0)
     for step in (16, 32, 64):
         g = g + pltpu.roll(g, step, 1)
-    g = jnp.where(lane < 16, g, jnp.where(lane == row + 16, 1.0, 0.0))
-    for k in range(PROBES - 1):
-        pivot_row = jnp.broadcast_to(g[k : k + 1], (16, 128))
-        column = jnp.broadcast_to(g[:, k : k + 1], (16, 128))
-        pivot = jnp.broadcast_to(pivot_row[:, k : k + 1], (16, 128))
-        g = g - jnp.where(row > k, column / pivot, 0.0) * pivot_row
-    diagonal = jnp.sum(jnp.where(lane == row, g, 0.0), axis=1, keepdims=True)
-    g = g / jnp.sqrt(diagonal)
-    factor_ref[...] = jnp.where(lane >= row, g, 0.0)[:, :16]
+    column = [jnp.broadcast_to(g[:, j : j + 1], (16, 128)) for j in range(PROBES)]
+    inverse = [jnp.where(row == j, 1.0, 0.0) for j in range(PROBES)]
+    pivots = jnp.ones((16, 128), F32)
+    for k in range(PROBES):
+        pivot = jnp.broadcast_to(column[k][k : k + 1], (16, 128))
+        pivots = jnp.where(row == k, pivot, pivots)
+        ratio = jnp.where(row > k, column[k] / pivot, 0.0)
+        for j in range(k + 1, PROBES):
+            column[j] = column[j] - ratio * jnp.broadcast_to(column[j][k : k + 1], (16, 128))
+        for j in range(k + 1):
+            inverse[j] = inverse[j] - ratio * jnp.broadcast_to(inverse[j][k : k + 1], (16, 128))
+    scale = 1.0 / jnp.sqrt(pivots)
+    factor = jnp.zeros((16, 128), F32)
     for j in range(PROBES):
-        inv_ref[j] = jnp.broadcast_to(g[:, 16 + j : 17 + j], (16, 128))
+        factor = jnp.where((lane == j) & (row <= j), column[j] * scale, factor)
+        inv_ref[j] = inverse[j] * scale
+    factor_ref[...] = factor[:, :16]
     for i in range(PROBES):
         value = jnp.broadcast_to(inv_ref[0, i : i + 1], (64, 128)) * img_ref[0]
         for j in range(1, i + 1):
             value = value + jnp.broadcast_to(inv_ref[j, i : i + 1], (64, 128)) * img_ref[j]
         out_ref[i] = value
-
-
-def call(kernel, out_shapes, scratch=(), smem=0, inputs=1, copies=0):
+        pltpu.make_async_copy(out_ref.at[i], out_hbm.at[i], sems.at[i]).start()
+    for i in range(PROBES):
+        pltpu.make_async_copy(out_ref.at[i], out_hbm.at[i], sems.at[i]).wait()
+
+
+def call(kernel, out_shapes, scratch=(), smem=0, inputs=1, copies=(), limit=40):
     out_shape = [jax.ShapeDtypeStruct(s, F32) for s in out_shapes]
     vmem = pl.BlockSpec(memory_space=pltpu.VMEM)
-    given = pl.BlockSpec(memory_space=pltpu.HBM) if copies else vmem
-    specs = [pl.BlockSpec(memory_space=pltpu.SMEM)] * smem + [given] * inputs
-    sems = [pltpu.SemaphoreType.DMA((copies,))] if copies else []
+    hbm = pl.BlockSpec(memory_space=pl.ANY)
+    specs = [pl.BlockSpec(memory_space=pltpu.SMEM)] * smem
+    specs += [hbm if len(copies) == 2 else vmem] * inputs
     return pl.pallas_call(
         kernel,
         out_shape=out_shape,
         in_specs=specs,
-        out_specs=[vmem] * len(out_shape),
-        scratch_shapes=[pltpu.VMEM(s, F32) for s in scratch] + sems,
-        compiler_params=pltpu.CompilerParams(vmem_limit_bytes=40 * 1024 * 1024),
+        out_specs=[hbm if copies else vmem] + [vmem] * (len(out_shape) - 1),
+        scratch_shapes=[pltpu.VMEM(s, F32) for s in scratch]
+        + [pltpu.SemaphoreType.DMA((n,)) for n in copies],
+        compiler_params=pltpu.CompilerParams(vmem_limit_bytes=limit * 1024 * 1024),
     )
 
 
 def on_device(log_perm, pressure, data_weight, probes):
     planes = [a.reshape(64, 128) for a in (log_perm, pressure, data_weight)]
     block = (64, 128)
-    scratch = [block, block, block, (16, 64, 128), block, (128, 128)]
-    (sent,) = call(pack_kernel, [(32, 56, 128)], scratch, inputs=4, copies=4)(
+    scratch = [block, block, block, (16, 64, 128), block, (5, 128, 128), (32, 56, 128)]
+    (sent,) = call(pack_kernel, [(32, 56, 128)], scratch, inputs=4, copies=(7, 32), limit=60)(
         *planes, probes.reshape(16, 64, 128)
     )
     got = lax.all_to_all(sent, ("gx", "gy"), 0, 0)
@@ -496,7 +526,11 @@
     (gram,) = call(spread_kernel, [(16, 2, 128)])(gram)
     gram = lax.all_to_all(gram, "gz", 0, 0)
     basis, factor = call(
-        finish_kernel, [(16, 64, 128), (16, 16)], [(16, 16, 128)], inputs=2
+        finish_kernel,
+        [(16, 64, 128), (16, 16)],
+        [(16, 16, 128), (16, 64, 128)],
+        inputs=2,
+        copies=(16,),
     )(gram, image_rows)
     return (basis.reshape(probes.shape), factor)
 

time: 127 us -> 124 us (0.976)
  local copies, waits for them, and re-layouts: 3.31 us -> 0 us
    unnamed x8 -> x0, local copies, waits for them, and re-layouts: 3.31 us -> none
where the time goes in v3:
time: 124 us
  blocking collectives  88.1 us (71%)
  Pallas kernels  17.7 us (14%)
  waiting for transfers between devices  9.29 us (7%)
  starting transfers between devices  8.11 us (7%)
    all_to_all x1, blocking collectives, on_device(): got = lax.all_to_all(sent, ('gx', 'gy'), 0, 0)  37.2 us
    all_to_all x1, blocking collectives, on_device(): gram = lax.all_to_all(gram, 'gz', 0, 0)  18.4 us
    all_to_all x1, blocking collectives, on_device(): back = lax.all_to_all(images.reshape(32, 32, 128), ('gx', 'gy'), 0, 0)  17.9 us
    all_to_all x1, blocking collectives, on_device(): gram = lax.all_to_all(gram, ('gx', 'gy'), 0, 0)  14.6 us
    pallas_call x1, Pallas kernels, on_device(): call(core_kernel, [(1024, 128)], scratch, smem=1, inputs=5)  9.9 us
    ppermute x1, starting transfers between devices, on_device(): from_below = lax.ppermute(high, ('gx', 'gy', 'gz'), up)  6.19 us
    ppermute x1, waiting for transfers between devices, on_device(): from_below = lax.ppermute(high, ('gx', 'gy', 'gz'), up)  4.92 us
    ppermute x1, waiting for transfers between devices, on_device(): from_above = lax.ppermute(low, ('gx', 'gy', 'gz'), down)  4.37 us
  transfers between devices with their start and end apart: 2, of which 2 were waited for; matrix products, arithmetic and copies ran while one was open for 0% of the time, Pallas kernels for 0%

profile of v3, /device:TPU:1, one launch (start us, length us, event | category | flops | bytes accessed | tf_op | source)
XLA Modules:
  0.0 123.9 jit_solution(10228745779739158332)
XLA Ops:
  0.6 2.5 %shard_map.59 = f32[32,56,128]{2,1,0:T(8,128)} custom-call(f32[64,128]{1,0:T(8,128)} %bitcast.12, f32[64,128]{1,0:T(8,128)} %bitcast.13, f32[64,128]{1,0:T(8,128)} %bitcast.14, f32[16,64,128]{2,1,0:T(8,128)} %bitcast.11), custom_call_target="tpu_custom_call" | custom-call | tf_op jit(solution)/shard_map/pallas_call | solution.py:491
  3.1 37.2 %all_to_all.20 = f32[32,56,128]{2,1,0:T(8,128)S(1)} all-to-all(f32[32,56,128]{2,1,0:T(8,128)} %shard_map.59), channel_id=1, replica_groups=mesh['gx'=8,'gy'=4,'gz'=16] {'gx','gy'}, dimensions={0} | all-to-all | bytes 1835008 | tf_op jit(solution)/shard_map/all_to_all | solution.py:494
  40.3 2.1 %shard_map.60 = (f32[8,16,8,128]{3,2,1,0:T(8,128)S(1)}, f32[8,16,8,128]{3,2,1,0:T(8,128)S(1)}, f32[4,16,8,128]{3,2,1,0:T(8,128)S(1)}, f32[140,8,128]{2,1,0:T(8,128)S(1)}, f32[140,8,128]{2,1,0:T(8,128)}) custom-call(f32[1792,128]{1,0:T(8,128)S(1)} %bitcast.9), custom_call_target="tpu_custom_call" | custom-call | tf_op jit(solution)/shard_map/pallas_call | solution.py:496
  42.3 6.2 %collective-permute-start = (f32[140,8,128]{2,1,0:T(8,128)}, f32[140,8,128]{2,1,0:T(8,128)S(1)}, u32[]{:S(2)}, u32[]{:S(2)}) collective-permute-start(f32[140,8,128]{2,1,0:T(8,128)} %get-tuple-element.11), channel_id=1, source_target_pairs={{0,16},{16,80},{80,96},{96,32},{32,48},{48,112},{112,64},{64,65},{... | collective-permute-start | bytes 1720328 | tf_op jit(solution)/shard_map/ppermute | solution.py:509
  48.5 1.9 %collective-permute-start.1 = (f32[140,8,128]{2,1,0:T(8,128)S(1)}, f32[140,8,128]{2,1,0:T(8,128)S(1)}, u32[]{:S(2)}, u32[]{:S(2)}) collective-permute-start(f32[140,8,128]{2,1,0:T(8,128)S(1)} %get-tuple-element.15), channel_id=1, source_target_pairs={{16,0},{80,16},{96,80},{32,96},{48,32},{112,48},{64,112},{65,64},{... | collective-permute-start | bytes 1720328 | tf_op jit(solution)/shard_map/ppermute | solution.py:510
  50.5 0.1 add_convert_fusion.edge_ref
  50.6 4.9 %collective-permute-done.lo_ref = f32[140,8,128]{2,1,0:T(8,128)S(1)} collective-permute-done((f32[140,8,128]{2,1,0:T(8,128)}, f32[140,8,128]{2,1,0:T(8,128)S(1)}, u32[]{:S(2)}, u32[]{:S(2)}) %collective-permute-start) | collective-permute-done | bytes 573472 | tf_op jit(solution)/shard_map/ppermute | solution.py:509
  55.5 4.4 %collective-permute-done.1.hi_ref = f32[140,8,128]{2,1,0:T(8,128)S(1)} collective-permute-done((f32[140,8,128]{2,1,0:T(8,128)S(1)}, f32[140,8,128]{2,1,0:T(8,128)S(1)}, u32[]{:S(2)}, u32[]{:S(2)}) %collective-permute-start.1) | collective-permute-done | bytes 573472 | tf_op jit(solution)/shard_map/ppermute | solution.py:510
  59.9 9.9 %shard_map.61 = f32[1024,128]{1,0:T(8,128)S(1)} custom-call(s32[2]{0:T(128)S(1)} %add_convert_fusion.edge_ref, f32[140,8,128]{2,1,0:T(8,128)S(1)} %collective-permute-done.lo_ref, f32[8,16,8,128]{3,2,1,0:T(8,128)S(1)} %get-tuple-element.12.s_own_ref, f32[8,16,8,128]{3,2,1,0:T(8,128)S(1)} %get-tuple-element.13.c_own_ref, ...), custom_call_target="tpu_custom_call" | custom-call | tf_op jit(solution)/shard_map/pallas_call | solution.py:518
  69.8 17.9 %all_to_all.21.in_ref = f32[32,32,128]{2,1,0:T(8,128)S(1)} all-to-all(f32[32,32,128]{2,1,0:T(8,128)S(1)} %bitcast.10), channel_id=1, replica_groups=mesh['gx'=8,'gy'=4,'gz'=16] {'gx','gy'}, dimensions={0} | all-to-all | bytes 1048576 | tf_op jit(solution)/shard_map/all_to_all | solution.py:521
  87.6 0.8 shard_map.62
  88.5 14.6 %all_to_all.22.in_ref = f32[32,2,128]{2,1,0:T(2,128)S(1)} all-to-all(f32[32,2,128]{2,1,0:T(2,128)S(1)} %get-tuple-element.16), channel_id=1, replica_groups=mesh['gx'=8,'gy'=4,'gz'=16] {'gx','gy'}, dimensions={0} | all-to-all | bytes 65536 | tf_op jit(solution)/shard_map/all_to_all | solution.py:525
  103.1 18.4 %all_to_all.23.gram_ref = f32[16,2,128]{2,1,0:T(2,128)S(1)} all-to-all(f32[16,2,128]{2,1,0:T(2,128)S(1)} %shard_map.63), channel_id=1, replica_groups=mesh['gx'=8,'gy'=4,'gz'=16] {'gz'}, dimensions={0} | all-to-all | bytes 32768 | tf_op jit(solution)/shard_map/all_to_all | solution.py:527
  121.5 2.4 %shard_map.64 = (f32[16,64,128]{2,1,0:T(8,128)}, f32[16,16]{1,0:T(8,128)}) custom-call(f32[16,2,128]{2,1,0:T(2,128)S(1)} %all_to_all.23.gram_ref, f32[16,64,128]{2,1,0:T(8,128)S(1)} %get-tuple-element.17.img_ref), custom_call_target="tpu_custom_call" | custom-call | tf_op jit(solution)/shard_map/pallas_call | solution.py:528
  (1 shorter events, 0.0 us)
Async XLA Ops:
  42.3 13.1 %collective-permute-start = (f32[140,8,128]{2,1,0:T(8,128)}, f32[140,8,128]{2,1,0:T(8,128)S(1)}, u32[]{:S(2)}, u32[]{:S(2)}) collective-permute-start(f32[140,8,128]{2,1,0:T(8,128)} %get-tuple-element.11), channel_id=1, source_target_pairs={{0,16},{16,80},{80,96},{96,32},{32,48},{48,112},{112,64},{64,65},{... | collective-permute-start | bytes 1720328 | tf_op jit(solution)/shard_map/ppermute | solution.py:509
  48.5 11.3 %collective-permute-start.1 = (f32[140,8,128]{2,1,0:T(8,128)S(1)}, f32[140,8,128]{2,1,0:T(8,128)S(1)}, u32[]{:S(2)}, u32[]{:S(2)}) collective-permute-start(f32[140,8,128]{2,1,0:T(8,128)S(1)} %get-tuple-element.15), channel_id=1, source_target_pairs={{16,0},{80,16},{96,80},{32,96},{48,32},{112,48},{64,112},{65,64},{... | collective-permute-start | bytes 1720328 | tf_op jit(solution)/shard_map/ppermute | solution.py:510

commit v4 on v3

--- a/solution.py
+++ b/solution.py
@@ -70,8 +70,8 @@
 
 
 def pack_kernel(
-    lp_hbm, pr_hbm, dw_hbm, v_hbm, out_hbm,
-    lp_ref, pr_ref, dw_ref, v_ref, perm_ref, mix_ref, out_ref, in_sems, out_sems,
+    lp_hbm, pr_hbm, dw_hbm, v_hbm, out_ref,
+    lp_ref, pr_ref, dw_ref, v_ref, perm_ref, mix_ref, in_sems,
 ):
     pairs = [(lp_hbm, lp_ref), (pr_hbm, pr_ref), (dw_hbm, dw_ref)]
     pairs += [(v_hbm.at[pl.ds(4 * q, 4)], v_ref.at[pl.ds(4 * q, 4)]) for q in range(4)]
@@ -104,7 +104,6 @@
             packed = paired(tiles[i], w)
             for q in range(4):
                 out_ref[dest[w][q], 32 + 8 * i : 40 + 8 * i] = packed
-    sends = []
     for q in range(4):
         copies[3 + q].wait()
         for yl in range(2):
@@ -114,14 +113,6 @@
             tile = mixed(fields, 3 + yl)
             for w in range(8):
                 out_ref[dest[w][q], 16 * yl : 16 * yl + 16] = tile[16 * w : 16 * w + 16]
-        for w in range(8):
-            at = dest[w][q]
-            sends.append(
-                pltpu.make_async_copy(out_ref.at[at], out_hbm.at[at], out_sems.at[8 * q + w])
-            )
-            sends[-1].start()
-    for send in sends:
-        send.wait()
 
 
 def widen(v, first):
@@ -467,29 +458,29 @@
         pltpu.make_async_copy(out_ref.at[i], out_hbm.at[i], sems.at[i]).wait()
 
 
-def call(kernel, out_shapes, scratch=(), smem=0, inputs=1, copies=(), limit=40):
+def call(kernel, out_shapes, scratch=(), smem=0, inputs=1, fetch=0, send=0):
     out_shape = [jax.ShapeDtypeStruct(s, F32) for s in out_shapes]
     vmem = pl.BlockSpec(memory_space=pltpu.VMEM)
     hbm = pl.BlockSpec(memory_space=pl.ANY)
-    specs = [pl.BlockSpec(memory_space=pltpu.SMEM)] * smem
-    specs += [hbm if len(copies) == 2 else vmem] * inputs
+    specs = [pl.BlockSpec(memory_space=pltpu.SMEM)] * smem + [hbm if fetch else vmem] * inputs
     return pl.pallas_call(
         kernel,
         out_shape=out_shape,
         in_specs=specs,
-        out_specs=[hbm if copies else vmem] + [vmem] * (len(out_shape) - 1),
+        out_specs=[hbm if send else vmem] + [vmem] * (len(out_shape) - 1),
         scratch_shapes=[pltpu.VMEM(s, F32) for s in scratch]
-        + [pltpu.SemaphoreType.DMA((n,)) for n in copies],
-        compiler_params=pltpu.CompilerParams(vmem_limit_bytes=limit * 1024 * 1024),
+        + [pltpu.SemaphoreType.DMA((n,)) for n in (fetch, send) if n],
+        compiler_params=pltpu.CompilerParams(vmem_limit_bytes=40 * 1024 * 1024),
     )
 
 
 def on_device(log_perm, pressure, data_weight, probes):
     planes = [a.reshape(64, 128) for a in (log_perm, pressure, data_weight)]
     block = (64, 128)
-    scratch = [block, block, block, (16, 64, 128), block, (5, 128, 128), (32, 56, 128)]
-    (sent,) = call(pack_kernel, [(32, 56, 128)], scratch, inputs=4, copies=(7, 32), limit=60)(
-        *planes, probes.reshape(16, 64, 128)
+    scratch = [block, block, block, (16, 64, 128), block, (5, 128, 128)]
+    fields = [*planes, probes.reshape(16, 64, 128)]
+    (sent,) = call(pack_kernel, [(32, 56, 128)], scratch, inputs=4, fetch=7)(
+        *[pltpu.with_memory_space_constraint(a, pltpu.HBM) for a in fields]
     )
     got = lax.all_to_all(sent, ("gx", "gy"), 0, 0)
     plane, msg = (8, WIN, 8, 128), (MSG, 8, 128)
@@ -530,7 +521,7 @@
         [(16, 64, 128), (16, 16)],
         [(16, 16, 128), (16, 64, 128)],
         inputs=2,
-        copies=(16,),
+        send=16,
     )(gram, image_rows)
     return (basis.reshape(probes.shape), factor)
 

time: 124 us -> 123 us (level)
  no operation moved by 1% of the time
where the time goes in v4:
time: 123 us
  blocking collectives  87.9 us (71%)
  Pallas kernels  16.7 us (14%)
  waiting for transfers between devices  9.29 us (8%)
  starting transfers between devices  8.1 us (7%)
    all_to_all x1, blocking collectives, on_device(): got = lax.all_to_all(sent, ('gx', 'gy'), 0, 0)  37 us
    all_to_all x1, blocking collectives, on_device(): gram = lax.all_to_all(gram, 'gz', 0, 0)  18.4 us
    all_to_all x1, blocking collectives, on_device(): back = lax.all_to_all(images.reshape(32, 32, 128), ('gx', 'gy'), 0, 0)  17.9 us
    all_to_all x1, blocking collectives, on_device(): gram = lax.all_to_all(gram, ('gx', 'gy'), 0, 0)  14.6 us
    pallas_call x1, Pallas kernels, on_device(): call(core_kernel, [(1024, 128)], scratch, smem=1, inputs=5)  9.9 us
    ppermute x1, starting transfers between devices, on_device(): from_below = lax.ppermute(high, ('gx', 'gy', 'gz'), up)  6.18 us
    ppermute x1, waiting for transfers between devices, on_device(): from_below = lax.ppermute(high, ('gx', 'gy', 'gz'), up)  4.92 us
    ppermute x1, waiting for transfers between devices, on_device(): from_above = lax.ppermute(low, ('gx', 'gy', 'gz'), down)  4.37 us
  transfers between devices with their start and end apart: 2, of which 2 were waited for; matrix products, arithmetic and copies ran while one was open for 0% of the time, Pallas kernels for 0%

profile of v4, /device:TPU:1, one launch (start us, length us, event | category | flops | bytes accessed | tf_op | source)
XLA Modules:
  0.0 122.8 jit_solution(11120563008127481262)
XLA Ops:
  0.6 1.5 %shard_map.59 = f32[32,56,128]{2,1,0:T(8,128)S(1)} custom-call(f32[64,128]{1,0:T(8,128)} %bitcast.12, f32[64,128]{1,0:T(8,128)} %bitcast.13, f32[64,128]{1,0:T(8,128)} %bitcast.14, f32[16,64,128]{2,1,0:T(8,128)} %bitcast.11), custom_call_target="tpu_custom_call" | custom-call | tf_op jit(solution)/shard_map/pallas_call | solution.py:482
  2.1 37.0 %all_to_all.20 = f32[32,56,128]{2,1,0:T(8,128)S(1)} all-to-all(f32[32,56,128]{2,1,0:T(8,128)S(1)} %shard_map.59), channel_id=1, replica_groups=mesh['gx'=8,'gy'=4,'gz'=16] {'gx','gy'}, dimensions={0} | all-to-all | bytes 1835008 | tf_op jit(solution)/shard_map/all_to_all | solution.py:485
  39.1 2.1 %shard_map.60 = (f32[8,16,8,128]{3,2,1,0:T(8,128)S(1)}, f32[8,16,8,128]{3,2,1,0:T(8,128)S(1)}, f32[4,16,8,128]{3,2,1,0:T(8,128)S(1)}, f32[140,8,128]{2,1,0:T(8,128)S(1)}, f32[140,8,128]{2,1,0:T(8,128)}) custom-call(f32[1792,128]{1,0:T(8,128)S(1)} %bitcast.9), custom_call_target="tpu_custom_call" | custom-call | tf_op jit(solution)/shard_map/pallas_call | solution.py:487
  41.1 6.2 %collective-permute-start = (f32[140,8,128]{2,1,0:T(8,128)}, f32[140,8,128]{2,1,0:T(8,128)S(1)}, u32[]{:S(2)}, u32[]{:S(2)}) collective-permute-start(f32[140,8,128]{2,1,0:T(8,128)} %get-tuple-element.11), channel_id=1, source_target_pairs={{0,16},{16,80},{80,96},{96,32},{32,48},{48,112},{112,64},{64,65},{... | collective-permute-start | bytes 1720328 | tf_op jit(solution)/shard_map/ppermute | solution.py:500
  47.3 1.9 %collective-permute-start.1 = (f32[140,8,128]{2,1,0:T(8,128)S(1)}, f32[140,8,128]{2,1,0:T(8,128)S(1)}, u32[]{:S(2)}, u32[]{:S(2)}) collective-permute-start(f32[140,8,128]{2,1,0:T(8,128)S(1)} %get-tuple-element.15), channel_id=1, source_target_pairs={{16,0},{80,16},{96,80},{32,96},{48,32},{112,48},{64,112},{65,64},{... | collective-permute-start | bytes 1720328 | tf_op jit(solution)/shard_map/ppermute | solution.py:501
  49.3 0.1 add_convert_fusion.edge_ref
  49.4 4.9 %collective-permute-done.lo_ref = f32[140,8,128]{2,1,0:T(8,128)S(1)} collective-permute-done((f32[140,8,128]{2,1,0:T(8,128)}, f32[140,8,128]{2,1,0:T(8,128)S(1)}, u32[]{:S(2)}, u32[]{:S(2)}) %collective-permute-start) | collective-permute-done | bytes 573472 | tf_op jit(solution)/shard_map/ppermute | solution.py:500
  54.3 4.4 %collective-permute-done.1.hi_ref = f32[140,8,128]{2,1,0:T(8,128)S(1)} collective-permute-done((f32[140,8,128]{2,1,0:T(8,128)S(1)}, f32[140,8,128]{2,1,0:T(8,128)S(1)}, u32[]{:S(2)}, u32[]{:S(2)}) %collective-permute-start.1) | collective-permute-done | bytes 573472 | tf_op jit(solution)/shard_map/ppermute | solution.py:501
  58.7 9.9 %shard_map.61 = f32[1024,128]{1,0:T(8,128)S(1)} custom-call(s32[2]{0:T(128)S(1)} %add_convert_fusion.edge_ref, f32[140,8,128]{2,1,0:T(8,128)S(1)} %collective-permute-done.lo_ref, f32[8,16,8,128]{3,2,1,0:T(8,128)S(1)} %get-tuple-element.12.s_own_ref, f32[8,16,8,128]{3,2,1,0:T(8,128)S(1)} %get-tuple-element.13.c_own_ref, ...), custom_call_target="tpu_custom_call" | custom-call | tf_op jit(solution)/shard_map/pallas_call | solution.py:509
  68.6 17.9 %all_to_all.21.in_ref = f32[32,32,128]{2,1,0:T(8,128)S(1)} all-to-all(f32[32,32,128]{2,1,0:T(8,128)S(1)} %bitcast.10), channel_id=1, replica_groups=mesh['gx'=8,'gy'=4,'gz'=16] {'gx','gy'}, dimensions={0} | all-to-all | bytes 1048576 | tf_op jit(solution)/shard_map/all_to_all | solution.py:512
  86.4 0.8 shard_map.62
  87.3 14.6 %all_to_all.22.in_ref = f32[32,2,128]{2,1,0:T(2,128)S(1)} all-to-all(f32[32,2,128]{2,1,0:T(2,128)S(1)} %get-tuple-element.16), channel_id=1, replica_groups=mesh['gx'=8,'gy'=4,'gz'=16] {'gx','gy'}, dimensions={0} | all-to-all | bytes 65536 | tf_op jit(solution)/shard_map/all_to_all | solution.py:516
  101.9 18.4 %all_to_all.23.gram_ref = f32[16,2,128]{2,1,0:T(2,128)S(1)} all-to-all(f32[16,2,128]{2,1,0:T(2,128)S(1)} %shard_map.63), channel_id=1, replica_groups=mesh['gx'=8,'gy'=4,'gz'=16] {'gz'}, dimensions={0} | all-to-all | bytes 32768 | tf_op jit(solution)/shard_map/all_to_all | solution.py:518
  120.3 2.4 %shard_map.64 = (f32[16,64,128]{2,1,0:T(8,128)}, f32[16,16]{1,0:T(8,128)}) custom-call(f32[16,2,128]{2,1,0:T(2,128)S(1)} %all_to_all.23.gram_ref, f32[16,64,128]{2,1,0:T(8,128)S(1)} %get-tuple-element.17.img_ref), custom_call_target="tpu_custom_call" | custom-call | tf_op jit(solution)/shard_map/pallas_call | solution.py:519
  (1 shorter events, 0.0 us)
Async XLA Ops:
  41.1 13.1 %collective-permute-start = (f32[140,8,128]{2,1,0:T(8,128)}, f32[140,8,128]{2,1,0:T(8,128)S(1)}, u32[]{:S(2)}, u32[]{:S(2)}) collective-permute-start(f32[140,8,128]{2,1,0:T(8,128)} %get-tuple-element.11), channel_id=1, source_target_pairs={{0,16},{16,80},{80,96},{96,32},{32,48},{48,112},{112,64},{64,65},{... | collective-permute-start | bytes 1720328 | tf_op jit(solution)/shard_map/ppermute | solution.py:500
  47.3 11.3 %collective-permute-start.1 = (f32[140,8,128]{2,1,0:T(8,128)S(1)}, f32[140,8,128]{2,1,0:T(8,128)S(1)}, u32[]{:S(2)}, u32[]{:S(2)}) collective-permute-start(f32[140,8,128]{2,1,0:T(8,128)S(1)} %get-tuple-element.15), channel_id=1, source_target_pairs={{16,0},{80,16},{96,80},{32,96},{48,32},{112,48},{64,112},{65,64},{... | collective-permute-start | bytes 1720328 | tf_op jit(solution)/shard_map/ppermute | solution.py:501

commit v5 on v4

v5 whole, which is shorter than its diff:
```python
import jax
import jax.numpy as jnp
from jax import lax
from jax.experimental import pallas as pl
from jax.experimental.pallas import tpu as pltpu
from jax.sharding import PartitionSpec as P

DEG = 4
SHIFT = 0.5
LOWER = 0.5
UPPER = 33.5
MID = (UPPER + LOWER) / 2.0
HALF = (UPPER - LOWER) / 2.0
RATIO = MID / HALF

PROBES = 16
CELLS = 32 * 64 * 2048
WIN = 16
HALO = 2 * DEG + 2
INNER = DEG + 1
ROWS = WIN + 2 * HALO
UNROLL = 16
MSG = 12 * HALO + 4 * INNER
F32 = jnp.float32

PATHS = (
    ((0, 0), (0, 1), (1, 1), (1, 2), (0, 2), (0, 3), (1, 3), (1, 0)),
    ((1, 0), (1, 1), (2, 1), (2, 2), (1, 2), (1, 3), (2, 3), (2, 0)),
)


def place(block, w, q):
    core, layer = block % 2, block // 2
    gx = (PATHS[core][w][0] + 2 * (q + layer)) % 8
    return gx, PATHS[core][w][1]


def placer():
    block = lax.axis_index("gz")
    core, layer = block % 2, block // 2

    def number(w, q):
        (x0, y0), (x1, y1) = PATHS[0][w], PATHS[1][w]
        gx = (x0 + core * (x1 - x0) + 2 * (q + layer)) % 8
        return gx * 4 + y0 + core * (y1 - y0)

    return number


def lane_sub():
    lane = lax.broadcasted_iota(jnp.int32, (8, 128), 1)
    return lane, lax.broadcasted_iota(jnp.int32, (8, 128), 0)


def swap_groups(v):
    last = v[0].ndim - 1
    lane = lax.broadcasted_iota(jnp.int32, v[0].shape, last)
    high, low = (lane & 64) == 0, (lane & 32) == 0
    u = [None] * 4
    for a in range(2):
        moved = pltpu.roll(jnp.where(high, v[a + 2], v[a]), 64, last)
        u[a] = jnp.where(high, v[a], moved)
        u[a + 2] = jnp.where(high, moved, v[a + 2])
    out = [None] * 4
    for a in (0, 2):
        out[a] = jnp.where(low, u[a], pltpu.roll(u[a + 1], 32, last))
        out[a + 1] = jnp.where(low, pltpu.roll(u[a], 96, last), u[a + 1])
    return out


def pack_kernel(
    lp_hbm, pr_hbm, dw_hbm, v_hbm, out_ref,
    lp_ref, pr_ref, dw_ref, v_ref, perm_ref, mix_ref, in_sems,
):
    pairs = [(lp_hbm, lp_ref), (pr_hbm, pr_ref), (dw_hbm, dw_ref)]
    pairs += [(v_hbm.at[pl.ds(4 * q, 4)], v_ref.at[pl.ds(4 * q, 4)]) for q in range(4)]
    copies = [pltpu.make_async_copy(a, b, in_sems.at[i]) for i, (a, b) in enumerate(pairs)]
    for copy in copies:
        copy.start()
    first = (lane_sub()[0] & 2) == 0
    number = placer()
    dest = [[number(w, q) for q in range(4)] for w in range(8)]

    def mixed(parts, at):
        for slot in range(4):
            mix_ref[at, pl.ds(slot, 32, stride=4), :] = parts[slot]
        return mix_ref[at].T

    def half(ref, yl):
        return ref[pl.ds(yl, 32, stride=2), :]

    def paired(tile, w):
        return jnp.where(first, tile[16 * w : 16 * w + 8], tile[16 * w + 8 : 16 * w + 16])

    for copy in copies[:3]:
        copy.wait()
    perm_ref[...] = jnp.exp(lp_ref[...])
    perm = [half(perm_ref, yl) for yl in range(2)]
    tiles = [mixed([perm[yl], half(pr_ref, yl)] * 2, yl) for yl in range(2)]
    tiles.append(mixed([half(dw_ref, 0), half(dw_ref, 1)] * 2, 2))
    for w in range(8):
        for i in range(3):
            packed = paired(tiles[i], w)
            for q in range(4):
                out_ref[dest[w][q], 32 + 8 * i : 40 + 8 * i] = packed
    for q in range(4):
        copies[3 + q].wait()
        for yl in range(2):
            fields = [
                perm[yl] * v_ref[4 * q + p, pl.ds(yl, 32, stride=2), :] for p in range(4)
            ]
            tile = mixed(fields, 3 + yl)
            for w in range(8):
                out_ref[dest[w][q], 16 * yl : 16 * yl + 16] = tile[16 * w : 16 * w + 16]


def widen(v, first):
    last = v.ndim - 1
    return jnp.where(first, v, pltpu.roll(v, 2, last)), jnp.where(first, pltpu.roll(v, 126, last), v)


def split(v, even):
    last = v.ndim - 1
    return jnp.where(even, v, pltpu.roll(v, 1, last)), jnp.where(even, pltpu.roll(v, 127, last), v)


def arrange_kernel(in_ref, s_ref, c_ref, w_ref, low_ref, high_ref):
    first = (lane_sub()[0] & 2) == 0

    def fetch(begin, count):
        got = [
            jnp.stack([in_ref[pl.ds(56 * g + begin + k, 8, stride=224), :] for k in range(count)])
            for g in range(4)
        ]
        return swap_groups(got)

    lift, pairs = WIN - HALO, HALO // 2
    for yl in range(2):
        for begin in range(0, WIN, 8):
            for x, v in enumerate(fetch(16 * yl + begin, 8)):
                n = 4 * yl + x
                s_ref[n, begin : begin + 8] = v
                for k in range(8):
                    z = begin + k
                    if z < HALO:
                        low_ref[HALO * n + z] = v[k]
                    if z >= lift:
                        high_ref[HALO * n + z - lift] = v[k]
        for x, v in enumerate(fetch(32 + 8 * yl, 8)):
            n = 4 * yl + x
            below, above = widen(v, first)
            c_ref[n, 0:8] = below
            c_ref[n, 8:16] = above
            c = [below[z] if z < 8 else above[z - 8] for z in range(WIN)]
            for k in range(pairs):
                at = 8 * HALO + pairs * n + k
                low_ref[at] = jnp.where(first, c[k], c[k + pairs])
                high_ref[at] = jnp.where(first, c[lift + k], c[lift + k + pairs])
    for x, v in enumerate(fetch(48, 8)):
        below, above = widen(v, first)
        w_ref[x, 0:8] = below
        w_ref[x, 8:16] = above
        at = 12 * HALO + INNER * x
        low_ref[at : at + INNER] = below[:INNER]
        high_ref[at : at + INNER] = above[8 - INNER :]


FX, FY, FZ, OWN, FAR, COEFS = 0, 8, 16, 24, 32, 38


def far(v):
    return (
        [pltpu.roll(v[n], 7, 1) for n in (0, 4)]
        + [pltpu.roll(v[n], 1, 1) for n in (3, 7)]
        + [pltpu.roll(v[n], 124, 2) for n in range(4)]
        + [pltpu.roll(v[n + 4], 4, 2) for n in range(4)]
    )


def coefficients(perm, press, above, a_ref, b_ref, begin, count):
    lane, sub = lane_sub()
    at, faces = slice(begin, begin + count), slice(begin, begin + above[0][0].shape[0])
    perm_far, press_far = far(perm), far(press)
    none = jnp.zeros((8, 128), F32)
    half = {}
    for n in range(8):
        x_begin = jnp.where(sub == 0, 0.5, 0.0) if n % 4 == 0 else none
        x_end = jnp.where(sub == 7, 0.5, 0.0) if n % 4 == 3 else none
        y_begin = jnp.where(lane < 4, 0.5, 0.0) if n < 4 else none
        y_end = jnp.where(lane >= 124, 0.5, 0.0) if n >= 4 else none
        outside = (x_begin + x_end) + (y_begin + y_end)
        half[n] = (0.5 - x_begin, 0.5 - y_begin)
        for field, field_far, out_ref, sign in (
            (perm, perm_far, a_ref, 1.0),
            (press, press_far, b_ref, -1.0),
        ):
            up = field[n + 1] if n % 4 < 3 else field_far[n // 4]
            out_ref[FX + n, at] = (0.5 - x_end) * (field[n] + sign * up)
            up = field[n + 4] if n < 4 else field_far[n]
            out_ref[FY + n, at] = (0.5 - y_end) * (field[n] + sign * up)
        over_perm, over_press = above[0][n], above[1][n]
        size = over_perm.shape[0]
        a_ref[FZ + n, faces] = 0.5 * (perm[n][:size] + over_perm)
        b_ref[FZ + n, faces] = 0.5 * (press[n][:size] - over_press)
        a_ref[OWN + n, at] = SHIFT + outside * perm[n]
        b_ref[OWN + n, at] = outside * press[n]
    for i, n in enumerate((0, 4, 0, 1, 2, 3)):
        side, k = (half[n][0], 2 + i) if i < 2 else (half[n][1], 6 + i)
        a_ref[FAR + i, at] = side * (perm[n] + perm_far[k])
        b_ref[FAR + i, at] = side * (press_far[k] - press[n])


def sweep(field_ref, begin, end, coef_ref, join, sign, inputs, finish):
    def part(up, down):
        return up - down if sign < 0 else up + down

    def rows(row, count):
        here, below = pl.ds(row, count), pl.ds(row - 1, count + 1)
        now = [field_ref[n, here] for n in range(8)]
        around = far(now)
        flow_x, back_x, flow_y, back_y = ([None] * 8 for _ in range(4))
        for n in range(8):
            up = now[n + 1] if n % 4 < 3 else around[n // 4]
            flow_x[n] = join(now[n], up) * coef_ref[FX + n, here]
            up = now[n + 4] if n < 4 else around[n]
            flow_y[n] = join(now[n], up) * coef_ref[FY + n, here]
        for n in range(8):
            if n % 4:
                back_x[n] = flow_x[n - 1]
            else:
                back_x[n] = join(around[2 + n // 4], now[n]) * coef_ref[FAR + n // 4, here]
            if n >= 4:
                back_y[n] = flow_y[n - 4]
            else:
                back_y[n] = join(around[8 + n], now[n]) * coef_ref[FAR + 2 + n, here]
        results = []
        for n in range(8):
            flow_z = join(field_ref[n, below], field_ref[n, pl.ds(row, count + 1)])
            flow_z = flow_z * coef_ref[FZ + n, below]
            total = coef_ref[OWN + n, here] * now[n] + part(flow_x[n], back_x[n])
            total = total + (part(flow_y[n], back_y[n]) + part(flow_z[1:], flow_z[:-1]))
            extra = [ref[n, here] for ref in inputs]
            results.append((n, finish(row, count, n, now[n], total, *extra)))
        for n, outs in results:
            for ref, value in outs:
                ref[n, here] = value

    steps, rest = divmod(end - begin, UNROLL)

    def body(i, carry):
        rows(begin + UNROLL * i, UNROLL)
        return carry

    lax.fori_loop(0, steps, body, 0)
    if rest:
        rows(end - rest, rest)


def add(a, b):
    return a + b


def minus(a, b):
    return a - b


def step_table():
    table, keep_now, take_now, weight_now = [], 0.0, 1.0 / MID, 1.0 / RATIO
    for _ in range(DEG):
        weight_next = 1.0 / (2.0 * RATIO - weight_now)
        keep, take = weight_next * weight_now, 2.0 * weight_next / HALF
        table.append((keep + take / take_now, take * keep_now / take_now, take))
        keep_now, take_now, weight_now = keep, take, weight_next
    return table


def direction_of(repeat, v, total, old):
    grow, drop, take = step_table()[repeat]
    direction = grow * v - take * total
    return direction - drop * old[0] if repeat else direction


def own_kernel(edge_ref, s_ref, c_ref, w_ref, a_ref, b_ref, perm_ref, wt_ref, e_ref):
    even = (lane_sub()[0] & 1) == 0
    for x in range(4):
        wt_ref[x], wt_ref[4 + x] = split(w_ref[x], even)
    for begin in range(0, WIN, 8):
        parts = [split(c_ref[n, begin : begin + 8], even) for n in range(8)]
        perm, press = [p[0] for p in parts], [p[1] for p in parts]
        more = begin + 8 < WIN
        if more:
            after = [split(c_ref[n, begin + 8 : begin + 9], even) for n in range(8)]
            above = [[jnp.concatenate([v[1:], u[i]]) for v, u in zip((perm, press)[i], after)] for i in range(2)]
        else:
            above = [[v[1:] for v in field] for field in (perm, press)]
        coefficients(perm, press, above, a_ref, b_ref, begin, 8)
        for n in range(8):
            perm_ref[n, begin : begin + 8] = perm[n]
            for row, end in ((0, edge_ref[0]), (WIN - 1, edge_ref[1])):
                if begin <= row < begin + 8:
                    extra = 0.5 * end.astype(F32)
                    a_ref[OWN + n, row] = a_ref[OWN + n, row] + extra * perm[n][row - begin]
                    b_ref[OWN + n, row] = b_ref[OWN + n, row] + extra * press[n][row - begin]

    directions = [e_ref.at[i] for i in range(DEG)]

    def start(row, count, n, v, total):
        return [(directions[0], total * (1.0 / MID))]

    sweep(s_ref, 1, WIN - 1, b_ref, add, -1, (), start)
    for repeat in range(DEG - 1):

        def finish(row, count, n, v, total, *old, i=repeat):
            return [(directions[i + 1], direction_of(i, v, total, old))]

        old = directions[repeat - 1 : repeat] if repeat else ()
        begin = 2 + repeat
        sweep(directions[repeat], begin, WIN - begin, a_ref, minus, -1, old, finish)


def core_kernel(
    edge_ref, lo_ref, s_own_ref, c_own_ref, a_own_ref, b_own_ref, perm_ref, wt_own_ref, e_own_ref, hi_ref,
    out_ref,
    a_ref, b_ref, wt_ref, s_ref, *e_refs,
):
    image_ref = e_refs[1]
    first, even = (lane_sub()[0] & 2) == 0, (lane_sub()[0] & 1) == 0
    top = HALO + WIN

    def halo(src_ref):
        pairs = HALO // 2
        perm, press = [], []
        for n in range(8):
            begin = 8 * HALO + pairs * n
            wide = widen(src_ref[begin : begin + pairs], first)
            both = split(jnp.concatenate(wide), even)
            perm.append(both[0])
            press.append(both[1])
        return perm, press

    def rim(row):
        both = [split(c_own_ref[n, row : row + 1], even) for n in range(8)]
        return [v[0] for v in both], [v[1] for v in both]

    for n in range(8):
        s_ref[n, HALO:top] = s_own_ref[n]
        s_ref[n, :HALO] = lo_ref[HALO * n : HALO * n + HALO]
        s_ref[n, top:] = hi_ref[HALO * n : HALO * n + HALO]
        wt_ref[n, INNER : INNER + WIN] = wt_own_ref[n]
    for src_ref, at in ((lo_ref, slice(0, INNER)), (hi_ref, slice(INNER + WIN, 2 * INNER + WIN))):
        for x in range(4):
            begin = 12 * HALO + INNER * x
            wt_ref[x, at], wt_ref[4 + x, at] = split(src_ref[begin : begin + INNER], even)

    perm, press = halo(lo_ref)
    above = [
        [jnp.concatenate([v[1:], u]) for v, u in zip(field, over)]
        for field, over in zip((perm, press), rim(0))
    ]
    coefficients(perm, press, above, a_ref, b_ref, 0, HALO)
    perm, press = halo(hi_ref)
    here = [
        [jnp.concatenate([u, v[:-1]]) for v, u in zip(field, under)]
        for field, under in zip((perm, press), rim(WIN - 1))
    ]
    coefficients(here[0], here[1], (perm, press), a_ref, b_ref, top - 1, HALO)
    for ref, own_ref in ((a_ref, a_own_ref), (b_ref, b_own_ref)):
        for i in range(COEFS):
            size = WIN - 1 if FZ <= i < OWN else WIN
            ref[i, HALO : HALO + size] = own_ref[i, :size]
        for n in range(8):
            for row, end in ((HALO - 1, 0), (top - 1, 1)):
                ref[FZ + n, row] = ref[FZ + n, row] * (1.0 - edge_ref[end].astype(F32))

    def solve(lowest, finish_last, known):
        for repeat in range(DEG):
            last = repeat == DEG - 1

            def finish(row, count, n, v, total, *old, i=repeat):
                direction = direction_of(i, v, total, old)
                if i < DEG - 1:
                    return [(e_refs[i + 1], direction)]
                iterate = direction + v
                for e in old:
                    iterate = iterate + e
                return finish_last(row, count, n, iterate)

            old = e_refs[repeat - 1 :: -1] if last else e_refs[repeat - 1 : repeat]
            old = old if repeat else ()
            begin = lowest + 1 + repeat
            ranges = [(begin, ROWS - begin)]
            if known and not last:
                ranges = around(begin)
                keep(repeat + 1, begin)
            for low, high in ranges:
                sweep(e_refs[repeat], low, high, a_ref, minus, -1, old, finish)

    def around(begin):
        return [(begin, begin + HALO), (ROWS - begin - HALO, ROWS - begin)]

    def keep(i, begin):
        for n in range(8):
            e_refs[i][n, begin + HALO : ROWS - begin - HALO] = e_own_ref[i, n, begin : WIN - begin]

    def start(row, count, n, v, total):
        return [(e_refs[0], total * (1.0 / MID))]

    keep(0, 1)
    for low, high in around(1):
        sweep(s_ref, low, high, b_ref, add, -1, (), start)
    skip = HALO - INNER

    def second(row, count, n, value):
        return [(e_refs[0], value * (wt_ref[n, pl.ds(row - skip, count)] * (1.0 / MID)))]

    solve(1, second, True)
    solve(skip, lambda row, count, n, value: [(s_ref, value)], False)

    def image(row, count, n, v, total):
        return [(image_ref, perm_ref[n, pl.ds(row - HALO, count)] * total)]

    sweep(s_ref, HALO, top, b_ref, minus, 1, (), image)

    for yl in range(2):
        for begin in range(0, WIN, 8):
            at = slice(HALO + begin, HALO + begin + 8)
            v = swap_groups([image_ref[4 * yl + x, at] for x in range(4)])
            for g in range(4):
                for k in range(8):
                    to = g * 2 * WIN + yl * WIN + begin + k
                    out_ref[pl.ds(to, 8, stride=8 * WIN), :] = v[g][k]


def gram_kernel(in_ref, img_ref, gram_ref, acc_ref, mix_ref):
    number = placer()
    for q in range(4):
        source = [number(w, q) for w in range(8)]
        for yl in range(2):
            rows = [in_ref[source[w], 16 * yl : 16 * yl + 16] for w in range(8)]
            mix_ref[yl] = jnp.concatenate(rows, axis=0).T
            for p in range(4):
                img_ref[4 * q + p, pl.ds(yl, 32, stride=2), :] = mix_ref[
                    yl, pl.ds(p, 32, stride=4), :
                ]
    for i in range(PROBES):
        a = [img_ref[i, 8 * k : 8 * k + 8] for k in range(8)]
        for j in range(i + 1):
            parts = [a[k] * img_ref[j, 8 * k : 8 * k + 8] for k in range(8)]
            while len(parts) > 1:
                parts = [parts[k] + parts[k + 1] for k in range(0, len(parts), 2)]
            begin = (16 * i + j) * 8
            acc_ref[begin : begin + 8] = parts[0]
            begin = (16 * j + i) * 8
            acc_ref[begin : begin + 8] = parts[0]
    sums = []
    for c in range(32):
        parts = [acc_ref[pl.ds(64 * c + s, 8, stride=8), :] for s in range(8)]
        while len(parts) > 1:
            parts = [parts[k] + parts[k + 1] for k in range(0, len(parts), 2)]
        sums.append(parts[0])
    total = lax.dot_general(
        jnp.ones((8, 128), F32),
        jnp.concatenate(sums, axis=0),
        (((1,), (1,)), ((), ())),
        precision=lax.Precision.HIGHEST,
        preferred_element_type=F32,
    )
    _, sub = lane_sub()
    tile = jnp.where(sub == 0, total[:, :128], total[:, 128:])
    for d in range(32):
        gram_ref[d] = tile[0:2]


def spread_kernel(in_ref, out_ref):
    total = jnp.sum(in_ref[...], axis=0)
    for d in range(16):
        out_ref[d] = total


def finish_kernel(gram_ref, img_ref, out_hbm, factor_ref, out_ref, sems):
    total = jnp.sum(gram_ref[...], axis=0) * (1.0 / CELLS)
    lane = lax.broadcasted_iota(jnp.int32, (16, 128), 1)
    row = lax.broadcasted_iota(jnp.int32, (16, 128), 0)
    g = jnp.concatenate(
        [jnp.broadcast_to(total[0:1], (8, 128)), jnp.broadcast_to(total[1:2], (8, 128))], axis=0
    )
    g = jnp.where((lane >> 4) == (row & 7), g, 0.0)
    for step in (16, 32, 64):
        g = g + pltpu.roll(g, step, 1)
    column = [jnp.broadcast_to(g[:, j : j + 1], (16, 128)) for j in range(PROBES)]
    inverse = [jnp.where(row == j, 1.0, 0.0) for j in range(PROBES)]
    factor = jnp.zeros((16, 128), F32)
    for k in range(PROBES):
        pivot = jnp.broadcast_to(column[k][k : k + 1], (16, 128))
        scale = 1.0 / jnp.sqrt(pivot)
        for j in range(k, PROBES):
            factor = jnp.where((lane == j) & (row == k), column[j] * scale, factor)
        value = None
        for j in range(k + 1):
            weight = jnp.broadcast_to(inverse[j][k : k + 1] * scale[:1], (64, 128))
            term = weight * img_ref[j]
            value = term if value is None else value + term
        out_ref[k] = value
        pltpu.make_async_copy(out_ref.at[k], out_hbm.at[k], sems.at[k]).start()
        ratio = jnp.where(row > k, column[k] / pivot, 0.0)
        for j in range(k + 1, PROBES):
            column[j] = column[j] - ratio * jnp.broadcast_to(column[j][k : k + 1], (16, 128))
        for j in range(k + 1):
            inverse[j] = inverse[j] - ratio * jnp.broadcast_to(inverse[j][k : k + 1], (16, 128))
    factor_ref[...] = factor[:, :16]
    for i in range(PROBES):
        pltpu.make_async_copy(out_ref.at[i], out_hbm.at[i], sems.at[i]).wait()


def call(kernel, out_shapes, scratch=(), smem=0, inputs=1, fetch=0, send=0, cost=0):
    out_shape = [jax.ShapeDtypeStruct(s, F32) for s in out_shapes]
    vmem = pl.BlockSpec(memory_space=pltpu.VMEM)
    hbm = pl.BlockSpec(memory_space=pl.ANY)
    specs = [pl.BlockSpec(memory_space=pltpu.SMEM)] * smem + [hbm if fetch else vmem] * inputs
    return pl.pallas_call(
        kernel,
        out_shape=out_shape,
        in_specs=specs,
        out_specs=[hbm if send else vmem] + [vmem] * (len(out_shape) - 1),
        scratch_shapes=[pltpu.VMEM(s, F32) for s in scratch]
        + [pltpu.SemaphoreType.DMA((n,)) for n in (fetch, send) if n],
        compiler_params=pltpu.CompilerParams(vmem_limit_bytes=40 * 1024 * 1024),
        cost_estimate=pl.CostEstimate(flops=cost, bytes_accessed=cost, transcendentals=0) if cost else None,
    )


def on_device(log_perm, pressure, data_weight, probes):
    planes = [a.reshape(64, 128) for a in (log_perm, pressure, data_weight)]
    block = (64, 128)
    scratch = [block, block, block, (16, 64, 128), block, (5, 128, 128)]
    fields = [*planes, probes.reshape(16, 64, 128)]
    (sent,) = call(pack_kernel, [(32, 56, 128)], scratch, inputs=4, fetch=7)(
        *[pltpu.with_memory_space_constraint(a, pltpu.HBM) for a in fields]
    )
    got = lax.all_to_all(sent, ("gx", "gy"), 0, 0)
    plane, msg = (8, WIN, 8, 128), (MSG, 8, 128)
    own_s, own_c, own_w, low, high = call(
        arrange_kernel, [plane, plane, (4, WIN, 8, 128), msg, msg]
    )(got.reshape(32 * 56, 128))

    blocks = lax.axis_size("gz")
    up = []
    for q in range(4):
        route = []
        for n in range(8 * blocks):
            gx, gy = place(n // 8, n % 8, q)
            route.append((gx * 4 + gy) * blocks + n // 8)
        up += [(route[n], route[n + 1]) for n in range(len(route) - 1)]
    down = [(j, i) for i, j in up]
    from_below = lax.ppermute(high, ("gx", "gy", "gz"), up)
    from_above = lax.ppermute(low, ("gx", "gy", "gz"), down)
    block = lax.axis_index("gz")
    at_end = (lax.axis_index("gx") % 2 == 0) & (lax.axis_index("gy") == 0)
    edge = jnp.stack([at_end & (block == 0), at_end & (block == blocks - 1)]).astype(jnp.int32)
    field, plane = (8, ROWS, 8, 128), (8, WIN, 8, 128)
    window, whole = (COEFS, WIN, 8, 128), (COEFS, ROWS, 8, 128)
    a_own, b_own, perm, weight, directions = call(
        own_kernel, [window, window, plane, plane, (DEG,) + plane], smem=1, inputs=3, cost=6_000_000
    )(edge, own_s, own_c, own_w)
    scratch = [whole] * 2 + [(8, WIN + 2 * INNER, 8, 128)] + [field] * 5
    (images,) = call(core_kernel, [(1024, 128)], scratch, smem=1, inputs=9)(
        edge, from_below, own_s, own_c, a_own, b_own, perm, weight, directions, from_above
    )
    back = lax.all_to_all(images.reshape(32, 32, 128), ("gx", "gy"), 0, 0)
    image_rows, gram = call(
        gram_kernel, [(16, 64, 128), (32, 2, 128)], [(2048, 128), (2, 128, 128)]
    )(back)
    gram = lax.all_to_all(gram, ("gx", "gy"), 0, 0)
    (gram,) = call(spread_kernel, [(16, 2, 128)])(gram)
    gram = lax.all_to_all(gram, "gz", 0, 0)
    basis, factor = call(
        finish_kernel,
        [(16, 64, 128), (16, 16)],
        [(16, 64, 128)],
        inputs=2,
        send=16,
    )(gram, image_rows)
    return (basis.reshape(probes.shape), factor)


def solution(mesh):
    in_specs = (
        P("gx", "gy", "gz"),
        P("gx", "gy", "gz"),
        P("gx", "gy", "gz"),
        P(None, "gx", "gy", "gz"),
    )
    out_specs = (P(None, "gx", "gy", "gz"), P())
    return jax.shard_map(
        on_device, mesh=mesh, in_specs=in_specs, out_specs=out_specs, check_vma=False
    )
```

time: 123 us -> 122 us (level)
  waiting for transfers between devices: 9.29 us -> 7.04 us
    ppermute x1, waiting for transfers between devices: 4.92 us -> 2.66 us  [on_device(): from_below = lax.ppermute(high, ('gx', 'gy', 'gz'), up)]
    pallas_call x2 -> x3, Pallas kernels: 12.3 us -> 13.2 us  [the longest x1 8.67 us: on_device(): call(core_kernel, [(1024, 128)], scratch, smem=1, inputs=9)]
  transfers between devices with their start and end apart: 2 -> 2, of which waited for: 2 -> 2; matrix products, arithmetic and copies ran while one was open for 0% -> 0% of each run, Pallas kernels for 0% -> 2%
where the time goes in v5:
time: 122 us; the launch traced here: 121 us
  blocking collectives  87.9 us (72%)
  Pallas kernels  17.6 us (14%)
  starting transfers between devices  8.1 us (7%)
  waiting for transfers between devices  7.04 us (6%)
    all_to_all x1, blocking collectives, on_device(): got = lax.all_to_all(sent, ('gx', 'gy'), 0, 0)  37 us
    all_to_all x1, blocking collectives, on_device(): gram = lax.all_to_all(gram, 'gz', 0, 0)  18.4 us
    all_to_all x1, blocking collectives, on_device(): back = lax.all_to_all(images.reshape(32, 32, 128), ('gx', 'gy'), 0, 0)  17.9 us
    all_to_all x1, blocking collectives, on_device(): gram = lax.all_to_all(gram, ('gx', 'gy'), 0, 0)  14.6 us
    pallas_call x1, Pallas kernels, on_device(): call(core_kernel, [(1024, 128)], scratch, smem=1, inputs=9)  8.67 us
    ppermute x1, starting transfers between devices, on_device(): from_below = lax.ppermute(high, ('gx', 'gy', 'gz'), up)  6.18 us
    ppermute x1, waiting for transfers between devices, on_device(): from_above = lax.ppermute(low, ('gx', 'gy', 'gz'), down)  4.37 us
    ppermute x1, waiting for transfers between devices, on_device(): from_below = lax.ppermute(high, ('gx', 'gy', 'gz'), up)  2.66 us
  transfers between devices with their start and end apart: 2, of which 2 were waited for; matrix products, arithmetic and copies ran while one was open for 0% of the time, Pallas kernels for 2%

profile of v5, /device:TPU:1, one launch (start us, length us, event | category | flops | bytes accessed | tf_op | source)
XLA Modules:
  0.0 121.4 jit_solution(7286708338859386728)
XLA Ops:
  0.6 1.5 %shard_map.59 = f32[32,56,128]{2,1,0:T(8,128)S(1)} custom-call(f32[64,128]{1,0:T(8,128)} %bitcast.12, f32[64,128]{1,0:T(8,128)} %bitcast.13, f32[64,128]{1,0:T(8,128)} %bitcast.14, f32[16,64,128]{2,1,0:T(8,128)} %bitcast.11), custom_call_target="tpu_custom_call" | custom-call | tf_op jit(solution)/shard_map/pallas_call | solution.py:537
  2.1 37.0 %all_to_all.20 = f32[32,56,128]{2,1,0:T(8,128)S(1)} all-to-all(f32[32,56,128]{2,1,0:T(8,128)S(1)} %shard_map.59), channel_id=1, replica_groups=mesh['gx'=8,'gy'=4,'gz'=16] {'gx','gy'}, dimensions={0} | all-to-all | bytes 1835008 | tf_op jit(solution)/shard_map/all_to_all | solution.py:540
  39.1 2.1 %shard_map.60 = (f32[8,16,8,128]{3,2,1,0:T(8,128)S(1)}, f32[8,16,8,128]{3,2,1,0:T(8,128)S(1)}, f32[4,16,8,128]{3,2,1,0:T(8,128)S(1)}, f32[140,8,128]{2,1,0:T(8,128)S(1)}, f32[140,8,128]{2,1,0:T(8,128)}) custom-call(f32[1792,128]{1,0:T(8,128)S(1)} %bitcast.9), custom_call_target="tpu_custom_call" | custom-call | tf_op jit(solution)/shard_map/pallas_call | solution.py:542
  41.2 6.2 %collective-permute-start = (f32[140,8,128]{2,1,0:T(8,128)}, f32[140,8,128]{2,1,0:T(8,128)S(1)}, u32[]{:S(2)}, u32[]{:S(2)}) collective-permute-start(f32[140,8,128]{2,1,0:T(8,128)} %get-tuple-element.16), channel_id=1, source_target_pairs={{0,16},{16,80},{80,96},{96,32},{32,48},{48,112},{112,64},{64,65},{... | collective-permute-start | bytes 1720328 | tf_op jit(solution)/shard_map/ppermute | solution.py:555
  47.3 1.9 %collective-permute-start.1 = (f32[140,8,128]{2,1,0:T(8,128)S(1)}, f32[140,8,128]{2,1,0:T(8,128)S(1)}, u32[]{:S(2)}, u32[]{:S(2)}) collective-permute-start(f32[140,8,128]{2,1,0:T(8,128)S(1)} %get-tuple-element.25), channel_id=1, source_target_pairs={{16,0},{80,16},{96,80},{32,96},{48,32},{112,48},{64,112},{65,64},{... | collective-permute-start | bytes 1720328 | tf_op jit(solution)/shard_map/ppermute | solution.py:556
  49.3 0.1 add_convert_fusion.edge_ref
  49.4 2.2 %shard_map.61 = (f32[38,16,8,128]{3,2,1,0:T(8,128)S(1)}, f32[38,16,8,128]{3,2,1,0:T(8,128)S(1)}, f32[8,16,8,128]{3,2,1,0:T(8,128)S(1)}, f32[8,16,8,128]{3,2,1,0:T(8,128)S(1)}, f32[4,8,16,8,128]{4,3,2,1,0:T(8,128)S(1)}) custom-call(s32[2]{0:T(128)S(1)} %add_convert_fusion.edge_ref, f32[8,16,8,128]{3,2,1,0:T(8,128)S(1)} %get-tuple-element.17.s_ref.s_own_ref, ...), custom_call_target="tpu_custom_call" | custom-call | flops 6000000 | bytes 6000000 | tf_op jit(solution)/shard_map/pallas_call | solution.py:562
  51.6 2.7 %collective-permute-done.lo_ref = f32[140,8,128]{2,1,0:T(8,128)S(1)} collective-permute-done((f32[140,8,128]{2,1,0:T(8,128)}, f32[140,8,128]{2,1,0:T(8,128)S(1)}, u32[]{:S(2)}, u32[]{:S(2)}) %collective-permute-start) | collective-permute-done | bytes 573472 | tf_op jit(solution)/shard_map/ppermute | solution.py:555
  54.3 4.4 %collective-permute-done.1.hi_ref = f32[140,8,128]{2,1,0:T(8,128)S(1)} collective-permute-done((f32[140,8,128]{2,1,0:T(8,128)S(1)}, f32[140,8,128]{2,1,0:T(8,128)S(1)}, u32[]{:S(2)}, u32[]{:S(2)}) %collective-permute-start.1) | collective-permute-done | bytes 573472 | tf_op jit(solution)/shard_map/ppermute | solution.py:556
  58.7 8.7 %shard_map.62 = f32[1024,128]{1,0:T(8,128)S(1)} custom-call(s32[2]{0:T(128)S(1)} %add_convert_fusion.edge_ref, f32[140,8,128]{2,1,0:T(8,128)S(1)} %collective-permute-done.lo_ref, f32[8,16,8,128]{3,2,1,0:T(8,128)S(1)} %get-tuple-element.17.s_ref.s_own_ref, f32[8,16,8,128]{3,2,1,0:T(8,128)S(1)} %get-tuple-element.18.c_ref.c_own_ref, ...), custom_call_target="tpu_custom_call" | custom-call | tf_op jit(solution)/shard_map/pallas_call | solution.py:566
  67.3 17.9 %all_to_all.21.in_ref = f32[32,32,128]{2,1,0:T(8,128)S(1)} all-to-all(f32[32,32,128]{2,1,0:T(8,128)S(1)} %bitcast.10), channel_id=1, replica_groups=mesh['gx'=8,'gy'=4,'gz'=16] {'gx','gy'}, dimensions={0} | all-to-all | bytes 1048576 | tf_op jit(solution)/shard_map/all_to_all | solution.py:569
  85.2 0.8 shard_map.63
  86.0 14.6 %all_to_all.22.in_ref = f32[32,2,128]{2,1,0:T(2,128)S(1)} all-to-all(f32[32,2,128]{2,1,0:T(2,128)S(1)} %get-tuple-element.26), channel_id=1, replica_groups=mesh['gx'=8,'gy'=4,'gz'=16] {'gx','gy'}, dimensions={0} | all-to-all | bytes 65536 | tf_op jit(solution)/shard_map/all_to_all | solution.py:573
  100.7 18.4 %all_to_all.23.gram_ref = f32[16,2,128]{2,1,0:T(2,128)S(1)} all-to-all(f32[16,2,128]{2,1,0:T(2,128)S(1)} %shard_map.64), channel_id=1, replica_groups=mesh['gx'=8,'gy'=4,'gz'=16] {'gz'}, dimensions={0} | all-to-all | bytes 32768 | tf_op jit(solution)/shard_map/all_to_all | solution.py:575
  119.1 2.3 %shard_map.65 = (f32[16,64,128]{2,1,0:T(8,128)}, f32[16,16]{1,0:T(8,128)}) custom-call(f32[16,2,128]{2,1,0:T(2,128)S(1)} %all_to_all.23.gram_ref, f32[16,64,128]{2,1,0:T(8,128)S(1)} %get-tuple-element.27.img_ref), custom_call_target="tpu_custom_call" | custom-call | tf_op jit(solution)/shard_map/pallas_call | solution.py:576
  (1 shorter events, 0.0 us)
Async XLA Ops:
  41.2 13.1 %collective-permute-start = (f32[140,8,128]{2,1,0:T(8,128)}, f32[140,8,128]{2,1,0:T(8,128)S(1)}, u32[]{:S(2)}, u32[]{:S(2)}) collective-permute-start(f32[140,8,128]{2,1,0:T(8,128)} %get-tuple-element.16), channel_id=1, source_target_pairs={{0,16},{16,80},{80,96},{96,32},{32,48},{48,112},{112,64},{64,65},{... | collective-permute-start | bytes 1720328 | tf_op jit(solution)/shard_map/ppermute | solution.py:555
  47.3 11.3 %collective-permute-start.1 = (f32[140,8,128]{2,1,0:T(8,128)S(1)}, f32[140,8,128]{2,1,0:T(8,128)S(1)}, u32[]{:S(2)}, u32[]{:S(2)}) collective-permute-start(f32[140,8,128]{2,1,0:T(8,128)S(1)} %get-tuple-element.25), channel_id=1, source_target_pairs={{16,0},{80,16},{96,80},{32,96},{48,32},{112,48},{64,112},{65,64},{... | collective-permute-start | bytes 1720328 | tf_op jit(solution)/shard_map/ppermute | solution.py:556

commit v6 on v5

--- a/solution.py
+++ b/solution.py
@@ -467,13 +467,13 @@
     )
     _, sub = lane_sub()
     tile = jnp.where(sub == 0, total[:, :128], total[:, 128:])
-    for d in range(32):
+    for d in range(16):
         gram_ref[d] = tile[0:2]
 
 
 def spread_kernel(in_ref, out_ref):
     total = jnp.sum(in_ref[...], axis=0)
-    for d in range(16):
+    for d in range(32):
         out_ref[d] = total
 
 
@@ -568,11 +568,11 @@
     )
     back = lax.all_to_all(images.reshape(32, 32, 128), ("gx", "gy"), 0, 0)
     image_rows, gram = call(
-        gram_kernel, [(16, 64, 128), (32, 2, 128)], [(2048, 128), (2, 128, 128)]
+        gram_kernel, [(16, 64, 128), (16, 2, 128)], [(2048, 128), (2, 128, 128)]
     )(back)
+    gram = lax.all_to_all(gram, "gz", 0, 0)
+    (gram,) = call(spread_kernel, [(32, 2, 128)])(gram)
     gram = lax.all_to_all(gram, ("gx", "gy"), 0, 0)
-    (gram,) = call(spread_kernel, [(16, 2, 128)])(gram)
-    gram = lax.all_to_all(gram, "gz", 0, 0)
     basis, factor = call(
         finish_kernel,
         [(16, 64, 128), (16, 16)],

time: 122 us -> 120 us (0.984)
  blocking collectives: 87.9 us -> 86.5 us
    all_to_all x1, blocking collectives: 14.6 us -> 12.6 us  [on_device(): gram = lax.all_to_all(gram, ('gx', 'gy'), 0, 0)]
where the time goes in v6:
time: 120 us
  blocking collectives  86.5 us (72%)
  Pallas kernels  17.6 us (15%)
  starting transfers between devices  8.1 us (7%)
  waiting for transfers between devices  7.04 us (6%)
    all_to_all x1, blocking collectives, on_device(): got = lax.all_to_all(sent, ('gx', 'gy'), 0, 0)  37 us
    all_to_all x1, blocking collectives, on_device(): gram = lax.all_to_all(gram, 'gz', 0, 0)  19.1 us
    all_to_all x1, blocking collectives, on_device(): back = lax.all_to_all(images.reshape(32, 32, 128), ('gx', 'gy'), 0, 0)  17.9 us
    all_to_all x1, blocking collectives, on_device(): gram = lax.all_to_all(gram, ('gx', 'gy'), 0, 0)  12.6 us
    pallas_call x1, Pallas kernels, on_device(): call(core_kernel, [(1024, 128)], scratch, smem=1, inputs=9)  8.67 us
    ppermute x1, starting transfers between devices, on_device(): from_below = lax.ppermute(high, ('gx', 'gy', 'gz'), up)  6.18 us
    ppermute x1, waiting for transfers between devices, on_device(): from_above = lax.ppermute(low, ('gx', 'gy', 'gz'), down)  4.37 us
    ppermute x1, waiting for transfers between devices, on_device(): from_below = lax.ppermute(high, ('gx', 'gy', 'gz'), up)  2.66 us
  transfers between devices with their start and end apart: 2, of which 2 were waited for; matrix products, arithmetic and copies ran while one was open for 0% of the time, Pallas kernels for 2%

profile of v6, /device:TPU:1, one launch (start us, length us, event | category | flops | bytes accessed | tf_op | source)
XLA Modules:
  0.0 120.0 jit_solution(1227686753783829395)
XLA Ops:
  0.6 1.5 %shard_map.59 = f32[32,56,128]{2,1,0:T(8,128)S(1)} custom-call(f32[64,128]{1,0:T(8,128)} %bitcast.12, f32[64,128]{1,0:T(8,128)} %bitcast.13, f32[64,128]{1,0:T(8,128)} %bitcast.14, f32[16,64,128]{2,1,0:T(8,128)} %bitcast.11), custom_call_target="tpu_custom_call" | custom-call | tf_op jit(solution)/shard_map/pallas_call | solution.py:537
  2.1 37.0 %all_to_all.20 = f32[32,56,128]{2,1,0:T(8,128)S(1)} all-to-all(f32[32,56,128]{2,1,0:T(8,128)S(1)} %shard_map.59), channel_id=1, replica_groups=mesh['gx'=8,'gy'=4,'gz'=16] {'gx','gy'}, dimensions={0} | all-to-all | bytes 1835008 | tf_op jit(solution)/shard_map/all_to_all | solution.py:540
  39.1 2.1 %shard_map.60 = (f32[8,16,8,128]{3,2,1,0:T(8,128)S(1)}, f32[8,16,8,128]{3,2,1,0:T(8,128)S(1)}, f32[4,16,8,128]{3,2,1,0:T(8,128)S(1)}, f32[140,8,128]{2,1,0:T(8,128)S(1)}, f32[140,8,128]{2,1,0:T(8,128)}) custom-call(f32[1792,128]{1,0:T(8,128)S(1)} %bitcast.9), custom_call_target="tpu_custom_call" | custom-call | tf_op jit(solution)/shard_map/pallas_call | solution.py:542
  41.2 6.2 %collective-permute-start = (f32[140,8,128]{2,1,0:T(8,128)}, f32[140,8,128]{2,1,0:T(8,128)S(1)}, u32[]{:S(2)}, u32[]{:S(2)}) collective-permute-start(f32[140,8,128]{2,1,0:T(8,128)} %get-tuple-element.16), channel_id=1, source_target_pairs={{0,16},{16,80},{80,96},{96,32},{32,48},{48,112},{112,64},{64,65},{... | collective-permute-start | bytes 1720328 | tf_op jit(solution)/shard_map/ppermute | solution.py:555
  47.3 1.9 %collective-permute-start.1 = (f32[140,8,128]{2,1,0:T(8,128)S(1)}, f32[140,8,128]{2,1,0:T(8,128)S(1)}, u32[]{:S(2)}, u32[]{:S(2)}) collective-permute-start(f32[140,8,128]{2,1,0:T(8,128)S(1)} %get-tuple-element.25), channel_id=1, source_target_pairs={{16,0},{80,16},{96,80},{32,96},{48,32},{112,48},{64,112},{65,64},{... | collective-permute-start | bytes 1720328 | tf_op jit(solution)/shard_map/ppermute | solution.py:556
  49.3 0.1 add_convert_fusion.edge_ref
  49.4 2.2 %shard_map.61 = (f32[38,16,8,128]{3,2,1,0:T(8,128)S(1)}, f32[38,16,8,128]{3,2,1,0:T(8,128)S(1)}, f32[8,16,8,128]{3,2,1,0:T(8,128)S(1)}, f32[8,16,8,128]{3,2,1,0:T(8,128)S(1)}, f32[4,8,16,8,128]{4,3,2,1,0:T(8,128)S(1)}) custom-call(s32[2]{0:T(128)S(1)} %add_convert_fusion.edge_ref, f32[8,16,8,128]{3,2,1,0:T(8,128)S(1)} %get-tuple-element.17.s_ref.s_own_ref, ...), custom_call_target="tpu_custom_call" | custom-call | flops 6000000 | bytes 6000000 | tf_op jit(solution)/shard_map/pallas_call | solution.py:562
  51.6 2.7 %collective-permute-done.lo_ref = f32[140,8,128]{2,1,0:T(8,128)S(1)} collective-permute-done((f32[140,8,128]{2,1,0:T(8,128)}, f32[140,8,128]{2,1,0:T(8,128)S(1)}, u32[]{:S(2)}, u32[]{:S(2)}) %collective-permute-start) | collective-permute-done | bytes 573472 | tf_op jit(solution)/shard_map/ppermute | solution.py:555
  54.3 4.4 %collective-permute-done.1.hi_ref = f32[140,8,128]{2,1,0:T(8,128)S(1)} collective-permute-done((f32[140,8,128]{2,1,0:T(8,128)S(1)}, f32[140,8,128]{2,1,0:T(8,128)S(1)}, u32[]{:S(2)}, u32[]{:S(2)}) %collective-permute-start.1) | collective-permute-done | bytes 573472 | tf_op jit(solution)/shard_map/ppermute | solution.py:556
  58.7 8.7 %shard_map.62 = f32[1024,128]{1,0:T(8,128)S(1)} custom-call(s32[2]{0:T(128)S(1)} %add_convert_fusion.edge_ref, f32[140,8,128]{2,1,0:T(8,128)S(1)} %collective-permute-done.lo_ref, f32[8,16,8,128]{3,2,1,0:T(8,128)S(1)} %get-tuple-element.17.s_ref.s_own_ref, f32[8,16,8,128]{3,2,1,0:T(8,128)S(1)} %get-tuple-element.18.c_ref.c_own_ref, ...), custom_call_target="tpu_custom_call" | custom-call | tf_op jit(solution)/shard_map/pallas_call | solution.py:566
  67.3 17.9 %all_to_all.21.in_ref = f32[32,32,128]{2,1,0:T(8,128)S(1)} all-to-all(f32[32,32,128]{2,1,0:T(8,128)S(1)} %bitcast.10), channel_id=1, replica_groups=mesh['gx'=8,'gy'=4,'gz'=16] {'gx','gy'}, dimensions={0} | all-to-all | bytes 1048576 | tf_op jit(solution)/shard_map/all_to_all | solution.py:569
  85.2 0.8 shard_map.63
  86.0 19.1 %all_to_all.22.in_ref = f32[16,2,128]{2,1,0:T(2,128)S(1)} all-to-all(f32[16,2,128]{2,1,0:T(2,128)S(1)} %get-tuple-element.26), channel_id=1, replica_groups=mesh['gx'=8,'gy'=4,'gz'=16] {'gz'}, dimensions={0} | all-to-all | bytes 32768 | tf_op jit(solution)/shard_map/all_to_all | solution.py:573
  105.1 12.6 %all_to_all.23.gram_ref = f32[32,2,128]{2,1,0:T(2,128)S(1)} all-to-all(f32[32,2,128]{2,1,0:T(2,128)S(1)} %shard_map.64), channel_id=1, replica_groups=mesh['gx'=8,'gy'=4,'gz'=16] {'gx','gy'}, dimensions={0} | all-to-all | bytes 65536 | tf_op jit(solution)/shard_map/all_to_all | solution.py:575
  117.7 2.3 %shard_map.65 = (f32[16,64,128]{2,1,0:T(8,128)}, f32[16,16]{1,0:T(8,128)}) custom-call(f32[32,2,128]{2,1,0:T(2,128)S(1)} %all_to_all.23.gram_ref, f32[16,64,128]{2,1,0:T(8,128)S(1)} %get-tuple-element.27.img_ref), custom_call_target="tpu_custom_call" | custom-call | tf_op jit(solution)/shard_map/pallas_call | solution.py:576
  (1 shorter events, 0.0 us)
Async XLA Ops:
  41.2 13.1 %collective-permute-start = (f32[140,8,128]{2,1,0:T(8,128)}, f32[140,8,128]{2,1,0:T(8,128)S(1)}, u32[]{:S(2)}, u32[]{:S(2)}) collective-permute-start(f32[140,8,128]{2,1,0:T(8,128)} %get-tuple-element.16), channel_id=1, source_target_pairs={{0,16},{16,80},{80,96},{96,32},{32,48},{48,112},{112,64},{64,65},{... | collective-permute-start | bytes 1720328 | tf_op jit(solution)/shard_map/ppermute | solution.py:555
  47.3 11.3 %collective-permute-start.1 = (f32[140,8,128]{2,1,0:T(8,128)S(1)}, f32[140,8,128]{2,1,0:T(8,128)S(1)}, u32[]{:S(2)}, u32[]{:S(2)}) collective-permute-start(f32[140,8,128]{2,1,0:T(8,128)S(1)} %get-tuple-element.25), channel_id=1, source_target_pairs={{16,0},{80,16},{96,80},{32,96},{48,32},{112,48},{64,112},{65,64},{... | collective-permute-start | bytes 1720328 | tf_op jit(solution)/shard_map/ppermute | solution.py:556
